TPU v7x, 256 devices: a whole 4x4x8 slice. The times are simulated.
256 devices in a mesh: seq: 32 (over z, x), head: 8 (over y, core).
Axes of the slice: x: 4, y: 4, z: 8, core: 2. Of those that a mesh axis runs over, the one named last changes fastest.
Arguments:
- query_states: bfloat16 [12288, 5120], P('seq', 'head')
- key_states: bfloat16 [12288, 5120], P('seq', 'head')
- value_states: bfloat16 [12288, 5120], P('seq', 'head')
- gate_states: bfloat16 [12288, 5120], P('seq', 'head'), may hold values from -8 to 8
- selection: int32 [192, 32], P('seq'), may hold values from 0 to 191, as said below
- out_weight: bfloat16 [5120, 5120], P('head'), may hold values from -0.078125 to 0.078125
Outputs:
- projected: bfloat16 [12288, 5120], P(('seq', 'head'))
Inputs may be any that keep to these rules, and one draw needn't show every extreme that they name: `selection`: each row names 32 different cubes. Taken together, the rows of one index of seq (aligned blocks of 6 rows) name at most 4 different cubes among the 6 cubes of any one index of seq, and exactly 4 of some index.
All inputs are finite; a program needn't handle non-finite values.
Results may differ from a plain program's by a relative error of at most 0.02.
Values may be sent and summed in bfloat16 or wider, within the bound.
A program may use at most 256 MiB of HBM per device.

v0:
```python
import jax
import jax.numpy as jnp
from jax import lax
from jax.sharding import PartitionSpec as P

HEAD_DIM = 128
CUBE = 64
TOPK = 32
CAP = 4


def soft_weights(scores):
    top = jnp.max(scores, axis=-1, keepdims=True)
    expo = jnp.exp(scores - top)
    return (expo / jnp.sum(expo, axis=-1, keepdims=True)).astype(jnp.bfloat16)


def body(query_states, key_states, value_states, gate_states, selection, out_weight):
    tok_rows = query_states.shape[0]
    feat_width = query_states.shape[1]
    head_count = feat_width // HEAD_DIM
    cube_dev = tok_rows // CUBE
    owner_count = lax.axis_size("seq")
    score_scale = HEAD_DIM ** (-0.5)
    pooled_key = jnp.mean(
        key_states.reshape(cube_dev, CUBE, feat_width), axis=1, dtype=jnp.float32
    ).astype(jnp.bfloat16)
    pooled_value = jnp.mean(
        value_states.reshape(cube_dev, CUBE, feat_width), axis=1, dtype=jnp.float32
    ).astype(jnp.bfloat16)
    matches = (
        selection[:, :, None] == jnp.arange(owner_count * cube_dev, dtype=jnp.int32)[None, None, :]
    )
    needed = jnp.any(matches, axis=(0, 1)).reshape(owner_count, cube_dev)
    slot_rank = jnp.cumsum(needed.astype(jnp.int32), axis=1) - 1
    placed = needed[:, :, None] & (
        slot_rank[:, :, None] == jnp.arange(CAP, dtype=jnp.int32)[None, None, :]
    )
    local_ids = jnp.arange(cube_dev, dtype=jnp.int32)
    request = jnp.sum(jnp.where(placed, local_ids[None, :, None], 0), axis=1)
    request = request + jnp.where(jnp.any(placed, axis=1), 0, cube_dev)
    asked_ids = lax.all_to_all(request, "seq", split_axis=0, concat_axis=0, tiled=True)
    all_key, all_value = (
        lax.all_gather(pooled_key, "seq", axis=0, tiled=True),
        lax.all_gather(pooled_value, "seq", axis=0, tiled=True),
    )
    cube_count = all_key.shape[0]
    queries = query_states.reshape(tok_rows, head_count, HEAD_DIM)
    coarse_scores = (
        jnp.einsum(
            "thd,khd->htk",
            queries,
            all_key.reshape(cube_count, head_count, HEAD_DIM),
            preferred_element_type=jnp.float32,
        )
        * score_scale
    )
    coarse_weight = soft_weights(coarse_scores)
    coarse_out = jnp.einsum(
        "htk,khd->thd",
        coarse_weight,
        all_value.reshape(cube_count, head_count, HEAD_DIM),
        preferred_element_type=jnp.float32,
    )
    blank_tile = jnp.zeros((1, CUBE, feat_width), jnp.bfloat16)
    key_store = jnp.concatenate(
        [key_states.reshape(cube_dev, CUBE, feat_width), blank_tile], axis=0
    )
    value_store = jnp.concatenate(
        [value_states.reshape(cube_dev, CUBE, feat_width), blank_tile], axis=0
    )
    key_send = key_store[asked_ids]
    value_send = value_store[asked_ids]
    slot_index = selection // cube_dev * CAP + slot_rank.reshape(-1)[selection]

    def arrange(tiles):
        flat_tiles = tiles.reshape(owner_count * CAP, CUBE, feat_width)
        return flat_tiles[slot_index].reshape(cube_dev, TOPK * CUBE, head_count, HEAD_DIM)

    cube_queries = query_states.reshape(cube_dev, CUBE, head_count, HEAD_DIM)
    got_keys, got_values = (
        lax.all_to_all(key_send, "seq", split_axis=0, concat_axis=0, tiled=True),
        lax.all_to_all(value_send, "seq", split_axis=0, concat_axis=0, tiled=True),
    )
    fine_scores = (
        jnp.einsum(
            "cqhd,ckhd->chqk", cube_queries, arrange(got_keys), preferred_element_type=jnp.float32
        )
        * score_scale
    )
    fine_weight = soft_weights(fine_scores)
    fine_out = jnp.einsum(
        "chqk,ckhd->cqhd", fine_weight, arrange(got_values), preferred_element_type=jnp.float32
    )
    fine_out = fine_out.reshape(tok_rows, head_count, HEAD_DIM)
    gates = jax.nn.sigmoid(gate_states.astype(jnp.float32)).reshape(tok_rows, head_count, HEAD_DIM)
    attended = (gates * (coarse_out + fine_out)).reshape(tok_rows, feat_width).astype(jnp.bfloat16)
    return lax.psum_scatter(
        jnp.dot(attended, out_weight, preferred_element_type=jnp.float32).astype(jnp.bfloat16),
        "head",
        scatter_dimension=0,
        tiled=True,
    )


def solution(mesh):
    placed = (
        P("seq", "head"),
        P("seq", "head"),
        P("seq", "head"),
        P("seq", "head"),
        P("seq", None),
        P("head", None),
    )
    return jax.shard_map(
        body, mesh=mesh, in_specs=placed, out_specs=P(("seq", "head"), None), check_vma=False
    )
```

profile of v0, /device:TPU:1, one launch (start us, length us, event | category | flops | bytes accessed | tf_op | source)
XLA Modules:
  0.0 834.0 jit_solution(14806534002548637865)
XLA Ops:
  8.6 11.9 %all-to-all-start = ((s32[32,1,4]{2,1,0:T(1,128)}), s32[32,1,4]{2,1,0:T(1,128)S(1)}, u32[]{:S(2)}, u32[]{:S(2)}) async-start(s32[32,1,4]{2,1,0:T(1,128)} %copy.43), calls=%async_computation | async-start | bytes 32768 | tf_op jit(solution)/shard_map/all_to_all | solution.py:42
  20.4 1.1 concatenate.7
  21.5 7.4 all-to-all-done
  29.2 7.6 gather_fusion.3
  36.9 5.1 all-to-all-start.2
  42.1 7.7 gather_fusion
  49.8 222.8 %all-to-all-done.2 = bf16[32,4,64,640]{3,2,1,0:T(8,128)(2,1)} async-done(((bf16[32,4,64,640]{3,2,1,0:T(8,128)(2,1)}), bf16[32,4,64,640]{3,2,1,0:T(8,128)(2,1)}, u32[]{:S(2)}, u32[]{:S(2)}) %all-to-all-start.2) | async-done | bytes 10485792 | tf_op jit(solution)/shard_map/all_to_all | solution.py:82
  272.6 20.1 %all-to-all-start.1 = ((bf16[32,4,64,640]{3,2,1,0:T(8,128)(2,1)}), bf16[32,4,64,640]{3,2,1,0:T(8,128)(2,1)}, u32[]{:S(2)}, u32[]{:S(2)}) async-start(bf16[32,4,64,640]{3,2,1,0:T(8,128)(2,1)} %bitcast.52), calls=%async_computation.1 | async-start | bytes 20971520 | tf_op jit(solution)/shard_map/all_to_all | solution.py:83
  294.5 1.6 gather_fusion.1
  296.4 270.0 %all-gather.1 = bf16[32,6,640]{2,1,0:T(8,128)(2,1)S(1)} all-gather(bf16[1,6,640]{2,1,0:T(8,128)(2,1)S(1)} %fusion.34), channel_id=1, replica_groups=mesh['seq'=32,'head'=8] {'seq'}, dimensions={0}, use_global_device_ids=true | all-gather | bytes 253440 | tf_op jit(solution)/shard_map/all_gather | solution.py:44
  567.5 34.3 %all-gather = bf16[32,6,640]{2,1,0:T(8,128)(2,1)S(1)} all-gather(bf16[1,6,640]{2,1,0:T(8,128)(2,1)S(1)} %fusion.33), channel_id=1, replica_groups=mesh['seq'=32,'head'=8] {'seq'}, dimensions={0}, use_global_device_ids=true | all-gather | bytes 253440 | tf_op jit(solution)/shard_map/all_gather | solution.py:45
  603.5 2.9 fusion.44
  606.4 13.8 %gather_fusion.4 = bf16[192,64,640]{2,1,0:T(8,128)(2,1)} fusion(bf16[128,64,640]{2,1,0:T(8,128)(2,1)} %bitcast.13, s32[1024]{0:T(1024)S(1)} %pad_clamp_fusion), kind=kCustom, calls=%fused_computation.4 | custom fusion | bytes 31458048 | tf_op jit(solution)/shard_map/gather | solution.py:78
  620.2 35.0 %reshape.111 = bf16[6,2048,5,128]{3,2,1,0:T(8,128)(2,1)} reshape(bf16[192,64,640]{2,1,0:T(8,128)(2,1)} %gather_fusion.4) | data formatting | bytes 31457280 | tf_op jit(solution)/shard_map/reshape | solution.py:78
  655.2 16.6 %fusion.6 = f32[6,5,2048,64]{2,3,1,0:T(8,128)} fusion(bf16[6,2048,5,128]{3,2,1,0:T(8,128)(2,1)} %reshape.111, bf16[6,64,5,128]{3,2,1,0:T(8,128)(2,1)S(1)} %reshape.112), kind=kOutput, calls=%fused_computation.13 | convolution fusion | flops 1006632960 | bytes 31948800 | tf_op jit(solution)/shard_map/cqhd,ckhd->chqk/dot_general | solution.py:86
  671.8 17.1 %fusion.43 = (f32[6,5,64]{2,1,0:T(8,128)S(1)}, f32[6,5,64,2048]{3,2,1,0:T(8,128)}) fusion(f32[6,5,2048,64]{2,3,1,0:T(8,128)} %fusion.6), kind=kOutput, calls=%fused_computation.63 | output fusion | flops 15730687 | bytes 31464960 | tf_op jit(solution)/shard_map/sub | solution.py:14
  688.9 13.6 %gather_fusion.2 = bf16[192,64,640]{2,1,0:T(8,128)(2,1)} fusion(bf16[128,64,640]{2,1,0:T(8,128)(2,1)} %bitcast.11, s32[1024]{0:T(1024)S(1)} %pad_clamp_fusion), kind=kCustom, calls=%fused_computation.2 | custom fusion | bytes 31458048 | tf_op jit(solution)/shard_map/gather | solution.py:78
  702.5 35.0 %reshape.109 = bf16[6,2048,5,128]{3,2,1,0:T(8,128)(2,1)} reshape(bf16[192,64,640]{2,1,0:T(8,128)(2,1)} %gather_fusion.2) | data formatting | bytes 31457280 | tf_op jit(solution)/shard_map/reshape | solution.py:78
  737.5 17.7 %fusion.20 = f32[6,64,5,128]{3,1,2,0:T(8,128)} fusion(bf16[6,2048,5,128]{3,2,1,0:T(8,128)(2,1)} %reshape.109, f32[6,5,64,2048]{3,2,1,0:T(8,128)} %get-tuple-element.6, f32[6,5,64]{2,1,0:T(8,128)S(1)} %get-tuple-element.5), kind=kOutput, calls=%fused_computation.29 | convolution fusion | flops 1014497280 | bytes 32448000 | tf_op jit(solution)/shard_map/chqk,ckhd->cqhd/dot_general | solution.py:92
  755.2 1.3 copy.49
  756.5 1.3 copy.50
  757.8 2.0 fusion.23
  759.8 8.0 convolution_convert_fusion
  767.9 59.3 %reduce-scatter.2.cloned.1.call-done = bf16[48,5120]{1,0:T(8,128)(2,1)} async-done(((bf16[384,5120]{1,0:T(8,128)(2,1)}), bf16[48,5120]{1,0:T(8,128)(2,1)}) %reduce-scatter.2.cloned.1.call-update) | async-done | bytes 491536 | tf_op jit(solution)/shard_map/reduce_scatter | solution.py:98
  (50 shorter events, 7.2 us)
Async XLA Ops:
  8.6 20.4 %all-to-all-start = ((s32[32,1,4]{2,1,0:T(1,128)}), s32[32,1,4]{2,1,0:T(1,128)S(1)}, u32[]{:S(2)}, u32[]{:S(2)}) async-start(s32[32,1,4]{2,1,0:T(1,128)} %copy.43), calls=%async_computation | async-start | bytes 32768 | tf_op jit(solution)/shard_map/all_to_all | solution.py:42
  36.9 5.1 copy-start.2
  36.9 235.7 %all-to-all-start.2 = ((bf16[32,4,64,640]{3,2,1,0:T(8,128)(2,1)}), bf16[32,4,64,640]{3,2,1,0:T(8,128)(2,1)}, u32[]{:S(2)}, u32[]{:S(2)}) async-start(bf16[32,4,64,640]{3,2,1,0:T(8,128)(2,1)} %bitcast.53), calls=%async_computation.2 | async-start | bytes 20971520 | tf_op jit(solution)/shard_map/all_to_all | solution.py:82
  49.7 243.1 %copy-start = (bf16[384,640]{1,0:T(8,128)(2,1)S(1)}, bf16[384,640]{1,0:T(8,128)(2,1)}, u32[]{:S(2)}) copy-start(bf16[384,640]{1,0:T(8,128)(2,1)} %param.6) | copy-start | bytes 1474564
  49.7 244.7 %copy-start.5 = (s32[6,32]{1,0:T(8,128)S(1)}, s32[6,32]{1,0:T(8,128)}, u32[]{:S(2)}) copy-start(s32[6,32]{1,0:T(8,128)} %param.10) | copy-start | bytes 2308
  49.8 246.5 %copy-start.1 = (bf16[384,640]{1,0:T(8,128)(2,1)S(1)}, bf16[384,640]{1,0:T(8,128)(2,1)}, u32[]{:S(2)}) copy-start(bf16[384,640]{1,0:T(8,128)(2,1)} %param.7) | copy-start | bytes 1474564
  49.8 553.2 %copy-start.3 = (bf16[384,640]{1,0:T(8,128)(2,1)S(1)}, bf16[384,640]{1,0:T(8,128)(2,1)}, u32[]{:S(2)}) copy-start(bf16[384,640]{1,0:T(8,128)(2,1)} %param.9) | copy-start | bytes 1474564
  272.6 416.3 %all-to-all-start.1 = ((bf16[32,4,64,640]{3,2,1,0:T(8,128)(2,1)}), bf16[32,4,64,640]{3,2,1,0:T(8,128)(2,1)}, u32[]{:S(2)}, u32[]{:S(2)}) async-start(bf16[32,4,64,640]{3,2,1,0:T(8,128)(2,1)} %bitcast.52), calls=%async_computation.1 | async-start | bytes 20971520 | tf_op jit(solution)/shard_map/all_to_all | solution.py:83
  292.7 534.5 %reduce-scatter.2.cloned.1.call-start = ((), (), s32[]{:S(2)}) async-start(), calls=%async_computation.4 | async-start | bytes 4423680 | tf_op jit(solution)/shard_map/reduce_scatter | solution.py:98
  737.5 20.3 %copy-start.4 = (bf16[192,5,128]{2,1,0:T(8,128)(2,1)S(1)}, bf16[192,5,128]{2,1,0:T(8,128)(2,1)}, u32[]{:S(2)}) copy-start(bf16[192,5,128]{2,1,0:T(8,128)(2,1)} %reshape.104) | copy-start | bytes 737284
Sparse Core Ops, SparseCore 0:
  768.0 59.1 reduce-scatter.1
where the time goes:
time: 838 us; the launch traced here: 834 us
  blocking collectives  304 us (36%)
  waiting for transfers between devices  290 us (35%)
  local copies, waits for them, and re-layouts  124 us (15%)
  matrix products  47.3 us (6%)
  starting transfers between devices  37.1 us (4%)
  other arithmetic  18.6 us (2%)
  between operations  13.6 us (2%)
    all_gather x1, blocking collectives, body(): lax.all_gather(pooled_key, 'seq', axis=0, tiled=True)  270 us
    all_to_all x1, waiting for transfers between devices, body(): lax.all_to_all(key_send, 'seq', split_axis=0, concat_axis=0, tiled=True)  223 us
    reshape x2, local copies, waits for them, and re-layouts, arrange(): flat_tiles[slot_index].reshape(cube_dev, TOPK * CUBE, head_count, HEAD_DIM)  70 us
    reduce_scatter x1, waiting for transfers between devices, body(): lax.psum_scatter(jnp.dot(attended, out_weight, preferred_element_type=jnp...  59.3 us
    all_gather x1, blocking collectives, body(): lax.all_gather(pooled_value, 'seq', axis=0, tiled=True)  34.3 us
    gather x2, local copies, waits for them, and re-layouts, arrange(): flat_tiles[slot_index].reshape(cube_dev, TOPK * CUBE, head_count, HEAD_DIM)  27.4 us
    all_to_all x1, starting transfers between devices, body(): lax.all_to_all(value_send, 'seq', split_axis=0, concat_axis=0, tiled=True)  20.1 us
    dot_general x1, matrix products, body(): jnp.einsum('chqk,ckhd->cqhd', fine_weight, arrange(got_values), preferred...  17.7 us
  transfers between devices with their start and end apart: 4, of which 3 were waited for; matrix products, arithmetic and copies ran while one was open for 12% of the time, Pallas kernels for 0%

commit v1 on v0

v1 whole, which is shorter than its diff:
```python
import functools
import math

import jax
import jax.numpy as jnp
from jax import lax
from jax.experimental import pallas as pl
from jax.experimental.pallas import tpu as pltpu
from jax.sharding import PartitionSpec as P

MESH = pl.DeviceIdType.MESH
HEAD_DIM = 128
CUBE = 64
CUBE_DEV = 6
TOPK = 32
NZ, NX = 8, 4
ROWS = CUBE * CUBE_DEV
HEADS_DEV = 5
ORDER = (0, 1, 7, 2, 6, 3, 5, 4)
XORDER = (1, 3, 2)
EXP_SCALE = HEAD_DIM ** (-0.5) * math.log2(math.e)


def place():
    seq, head = lax.axis_index("seq"), lax.axis_index("head")
    return seq // NX, seq % NX, head // 2, head % 2


def remote(src, dst, send_sem, recv_sem, seq, head):
    return pltpu.make_async_remote_copy(
        src_ref=src,
        dst_ref=dst,
        send_sem=send_sem,
        recv_sem=recv_sem,
        device_id={"seq": seq, "head": head},
        device_id_type=MESH,
    )


def arrived(ref, sem):
    pltpu.make_async_copy(ref, ref, sem).wait()


def greet(z, x, y, c):
    barrier = pltpu.get_barrier_semaphore()
    for dz in range(NZ):
        for dc in range(2):
            if dz or dc:
                pl.semaphore_signal(
                    barrier,
                    inc=1,
                    device_id={"seq": (z + dz) % NZ * NX + x, "head": 2 * y + (c + dc) % 2},
                    device_id_type=MESH,
                )
    for dx in range(1, NX):
        pl.semaphore_signal(
            barrier,
            inc=1,
            device_id={"seq": z * NX + (x + dx) % NX, "head": 2 * y + c},
            device_id_type=MESH,
        )
    pl.semaphore_wait(barrier, 2 * NZ - 1 + NX - 1)


def spread_kernel(
    q_ref, k_ref, v_ref, kv_ref, qf_ref, qr_ref,
    z_send, z_recv, x_send, x_recv, xq_send, xq_recv, c_send, c_recv,
):
    z, x, y, c = place()
    here = z * NX + x
    sibling = 2 * y + 1 - c
    main_slot = x + x // 3
    extra_slot = 4 - x // 3
    has_extra = z % 4 != 3
    member = (x != 3) | has_extra
    greet(z, x, y, c)

    def z_copies(act):
        for n, dz in enumerate(ORDER):
            zt = (z + dz) % NZ
            for cc in range(2):
                source = k_ref if cc == 0 else v_ref

                def one(cond, kind, src, dst):
                    def away():
                        copy = remote(
                            src, dst, z_send.at[n, cc, kind], z_recv.at[z, kind], zt * NX + x, 2 * y + cc
                        )
                        if act == "start":
                            copy.start()
                        else:
                            copy.wait_send()

                    if dz:
                        pl.when(cond)(away)
                    else:
                        pl.when(cond & (c != cc))(away)
                        if act == "start":
                            pl.when(cond & (c == cc))(
                                lambda: pltpu.make_async_copy(src, dst, z_recv.at[z, kind]).start()
                            )

                is_main = c == zt // 5
                col = pl.ds(pl.multiple_of(zt % 5 * HEAD_DIM, HEAD_DIM), HEAD_DIM)
                one(is_main, 0, source.at[:, col], kv_ref.at[cc, main_slot, z])
                is_extra = (c == 1) & (zt % 4 != 3)
                xcol = pl.ds(pl.multiple_of((3 + zt // 4) * HEAD_DIM, HEAD_DIM), HEAD_DIM)
                one(is_extra, 1, source.at[:, xcol], kv_ref.at[cc, extra_slot, z])
                one(is_main, 2, q_ref.at[:, cc, :, col], qr_ref.at[pl.ds(0, 3), z])
                rank = zt % 4 - zt % 4 // 3
                one(is_extra, 3, q_ref.at[rank, cc, :, xcol], qr_ref.at[3, z])

    z_copies("start")

    def x_copies(n, zs, act):
        for dx in XORDER:
            xt = (x + dx) % NX
            slot = main_slot + xt // 3 * (4 - main_slot)

            def away():
                copy = remote(
                    kv_ref.at[c, slot, zs], kv_ref.at[c, x, zs],
                    x_send.at[dx, n], x_recv.at[x, zs], z * NX + xt, 2 * y + c,
                )
                if act == "start":
                    copy.start()
                else:
                    copy.wait_send()

            pl.when((xt != 3) | has_extra)(away)

    def core_copy(xs, zs):
        return remote(
            kv_ref.at[c, xs, zs], kv_ref.at[c, xs, zs],
            c_send.at[xs, zs], c_recv.at[xs, zs], here, sibling,
        )

    def take_x(zs):
        for dx in XORDER:
            xs = (x + dx) % NX

            @pl.when(member)
            def _():
                arrived(kv_ref.at[c, xs, zs], x_recv.at[xs, zs])
                core_copy(xs, zs).start()

    lag = 2
    for n, dz in enumerate(ORDER):
        zs = (z + dz) % NZ
        arrived(kv_ref.at[c, main_slot, zs], z_recv.at[zs, 0])
        pl.when(has_extra)(lambda: arrived(kv_ref.at[c, extra_slot, zs], z_recv.at[zs, 1]))
        x_copies(n, zs, "start")
        pl.when(member)(lambda: core_copy(x, zs).start())
        if n >= lag:
            take_x((z + ORDER[n - lag]) % NZ)

    for zs in range(NZ):
        arrived(qr_ref.at[pl.ds(0, 3), zs], z_recv.at[zs, 2])
        pl.when(has_extra)(lambda: arrived(qr_ref.at[3, zs], z_recv.at[zs, 3]))

    def xq_copies(act):
        for dx in range(NX):
            xt = (x + dx) % NX

            def away():
                if dx:
                    copy = remote(
                        qr_ref.at[xt], qf_ref.at[x], xq_send.at[dx], xq_recv.at[x], z * NX + xt, 2 * y + c
                    )
                    if act == "start":
                        copy.start()
                    else:
                        copy.wait_send()
                elif act == "start":
                    pltpu.make_async_copy(qr_ref.at[x], qf_ref.at[x], xq_recv.at[x]).start()

            pl.when((xt != 3) | has_extra)(away)

    xq_copies("start")
    for n in range(NZ - lag, NZ):
        take_x((z + ORDER[n]) % NZ)

    @pl.when(member)
    def _():
        for xs in range(NX):
            arrived(qf_ref.at[xs], xq_recv.at[xs])
        for xs in range(NX):
            for zs in range(NZ):
                arrived(kv_ref.at[1 - c, xs, zs], c_recv.at[xs, zs])
                core_copy(xs, zs).wait_send()

    z_copies("wait")
    for n, dz in enumerate(ORDER):
        x_copies(n, (z + dz) % NZ, "wait")
    xq_copies("wait")


def spread(query_states, key_states, value_states):
    bf16 = jnp.bfloat16
    any_spec = pl.BlockSpec(memory_space=pl.ANY)
    dma = pltpu.SemaphoreType.DMA
    kv, qf, _ = pl.pallas_call(
        spread_kernel,
        out_shape=(
            jax.ShapeDtypeStruct((2, 5, NZ, ROWS, HEAD_DIM), bf16),
            jax.ShapeDtypeStruct((NX, NZ, CUBE, HEAD_DIM), bf16),
            jax.ShapeDtypeStruct((NX, NZ, CUBE, HEAD_DIM), bf16),
        ),
        in_specs=[any_spec] * 3,
        out_specs=(any_spec,) * 3,
        scratch_shapes=[
            dma((NZ, 2, 4)), dma((NZ, 4)),
            dma((NX, NZ)), dma((NX, NZ)),
            dma((NX,)), dma((NX,)),
            dma((NX, NZ)), dma((NX, NZ)),
        ],
        compiler_params=pltpu.CompilerParams(collective_id=0, has_side_effects=True),
        name="spread",
    )(query_states.reshape(3, 2, CUBE, HEADS_DEV * HEAD_DIM), key_states, value_states)
    return kv, qf


def collect_kernel(o_ref, a_ref, relay_ref, x_send, x_recv, z_send, z_recv):
    z, x, y, c = place()
    has_extra = z % 4 != 3
    member = (x != 3) | has_extra
    greet(z, x, y, c)

    def x_copies(act):
        for dx in range(NX):
            xt = (x + dx) % NX
            if dx:
                copy = remote(
                    o_ref.at[xt], relay_ref.at[x], x_send.at[dx], x_recv.at[x], z * NX + xt, 2 * y + c
                )
                if act == "start":
                    copy.start()
                else:
                    copy.wait_send()
            elif act == "start":
                pltpu.make_async_copy(o_ref.at[x], relay_ref.at[x], x_recv.at[x]).start()

    pl.when(member)(lambda: x_copies("start"))
    for xs in range(3):
        arrived(relay_ref.at[xs], x_recv.at[xs])
    pl.when(has_extra)(lambda: arrived(relay_ref.at[3], x_recv.at[3]))

    def z_copies(act):
        for n, dz in enumerate(ORDER):
            zt = (z + dz) % NZ

            def one(cond, kind, core, src, dst):
                def away():
                    copy = remote(
                        src, dst, z_send.at[n, kind], z_recv.at[z, c, kind], zt * NX + x, 2 * y + core
                    )
                    if act == "start":
                        copy.start()
                    else:
                        copy.wait_send()

                if dz:
                    pl.when(cond)(away)
                else:
                    pl.when(cond & (c != core))(away)
                    if act == "start":
                        pl.when(cond & (c == core))(
                            lambda: pltpu.make_async_copy(src, dst, z_recv.at[z, c, kind]).start()
                        )

            col = pl.ds(pl.multiple_of(z % 5 * HEAD_DIM, HEAD_DIM), HEAD_DIM)
            one(z >= 0, 0, z // 5, relay_ref.at[pl.ds(0, 3), zt], a_ref.at[:, c, :, col])
            xcol = pl.ds(pl.multiple_of((3 + z // 4) * HEAD_DIM, HEAD_DIM), HEAD_DIM)
            rank = z % 4 - z % 4 // 3
            one(has_extra, 1, 1, relay_ref.at[3, zt], a_ref.at[rank, c, :, xcol])

    z_copies("start")
    for zs in range(NZ):
        for cc in range(2):
            col = pl.ds(zs % 5 * HEAD_DIM, HEAD_DIM)
            pl.when(c == zs // 5)(lambda: arrived(a_ref.at[:, cc, :, col], z_recv.at[zs, cc, 0]))
            if zs % 4 != 3:
                xcol = pl.ds((3 + zs // 4) * HEAD_DIM, HEAD_DIM)
                pl.when(c == 1)(lambda: arrived(a_ref.at[zs % 4, cc, :, xcol], z_recv.at[zs, cc, 1]))
    pl.when(member)(lambda: x_copies("wait"))
    z_copies("wait")


def collect(outputs):
    bf16 = jnp.bfloat16
    any_spec = pl.BlockSpec(memory_space=pl.ANY)
    dma = pltpu.SemaphoreType.DMA
    attended, _ = pl.pallas_call(
        collect_kernel,
        out_shape=(
            jax.ShapeDtypeStruct((3, 2, CUBE, HEADS_DEV * HEAD_DIM), bf16),
            jax.ShapeDtypeStruct((NX, NZ, CUBE, HEAD_DIM), bf16),
        ),
        in_specs=[any_spec],
        out_specs=(any_spec,) * 2,
        scratch_shapes=[dma((NX,)), dma((NX,)), dma((NZ, 2)), dma((NZ, 2, 2))],
        compiler_params=pltpu.CompilerParams(collective_id=1, has_side_effects=True),
        name="collect",
    )(outputs)
    return attended.reshape(ROWS, HEADS_DEV * HEAD_DIM)


CONTRACT_LAST = (((1,), (1,)), ((), ()))
N_CUBES = NZ * NX * CUBE_DEV


def attend_kernel(sel_ref, kv_ref, q_ref, o_ref, pooled, scores):
    f32, bf16 = jnp.float32, jnp.bfloat16

    def pool(i, _):
        for a in range(2):
            block = kv_ref[a, pl.ds(pl.multiple_of(i * 1024, 1024), 1024), :].astype(f32)
            sums = jnp.sum(block.reshape(16, CUBE, HEAD_DIM), axis=1)
            pooled[a, pl.ds(pl.multiple_of(i * 16, 16), 16), :] = (sums * (1.0 / CUBE)).astype(bf16)
        return 0

    lax.fori_loop(0, N_CUBES // 16, pool, 0)
    group = 4
    width = group * CUBE

    def rows(a, t, g):
        tiles = [
            kv_ref[a, pl.ds(pl.multiple_of(sel_ref[t, g * group + n] * CUBE, CUBE), CUBE), :]
            for n in range(group)
        ]
        return jnp.concatenate(tiles, axis=0)

    def score(t, u):
        q = q_ref[t]
        top = None
        for g in range(TOPK // group):
            s = lax.dot_general(q, rows(0, t, g), CONTRACT_LAST, preferred_element_type=f32)
            scores[u, :, g * width:(g + 1) * width] = s
            part = jnp.maximum(s[:, :128], s[:, 128:])
            top = part if top is None else jnp.maximum(top, part)
        return q, jnp.max(top, axis=1, keepdims=True)

    def mix(t, u, q, top):
        acc = jnp.zeros((CUBE, HEAD_DIM), f32)
        total = jnp.zeros((CUBE, 128), f32)
        for g in range(TOPK // group):
            s = scores[u, :, g * width:(g + 1) * width]
            e = jnp.exp2((s - top) * EXP_SCALE)
            total = total + (e[:, :128] + e[:, 128:])
            acc = acc + jnp.dot(e.astype(bf16), rows(1, t, g), preferred_element_type=f32)
        fine = acc / jnp.sum(total, axis=1, keepdims=True)
        s = lax.dot_general(q, pooled[0], CONTRACT_LAST, preferred_element_type=f32)
        e = jnp.exp2((s - jnp.max(s, axis=1, keepdims=True)) * EXP_SCALE)
        coarse = jnp.dot(e.astype(bf16), pooled[1], preferred_element_type=f32)
        coarse = coarse / jnp.sum(e, axis=1, keepdims=True)
        o_ref[t] = (fine + coarse).astype(bf16)

    unroll = 2

    def step(i, _):
        held = [score(i * unroll + u, u) for u in range(unroll)]
        for u in range(unroll):
            mix(i * unroll + u, u, *held[u])
        return 0

    lax.fori_loop(0, NZ * NX // unroll, step, 0)


def attend(positions, kv, queries):
    bf16 = jnp.bfloat16
    whole = lambda *shape: pl.BlockSpec(shape, lambda i: (0,) * len(shape))
    return pl.pallas_call(
        attend_kernel,
        grid=(1,),
        out_shape=jax.ShapeDtypeStruct((NZ * NX, CUBE, HEAD_DIM), bf16),
        in_specs=[
            pl.BlockSpec(memory_space=pltpu.SMEM),
            whole(2, NZ * NX * ROWS, HEAD_DIM),
            whole(NZ * NX, CUBE, HEAD_DIM),
        ],
        out_specs=whole(NZ * NX, CUBE, HEAD_DIM),
        scratch_shapes=[
            pltpu.VMEM((2, N_CUBES, HEAD_DIM), bf16),
            pltpu.VMEM((2, CUBE, TOPK * CUBE), jnp.float32),
        ],
        compiler_params=pltpu.CompilerParams(vmem_limit_bytes=48 * 2**20),
        name="attend",
    )(positions, kv, queries)


def my_positions(selection):
    z, x, _, c = place()
    everyone = lax.all_gather(selection, "seq", axis=0, tiled=True)
    rank = x + x // 3 * (z % 4 - x)
    cube = jnp.minimum(2 * rank + c, CUBE_DEV - 1)
    mine = lax.dynamic_index_in_dim(everyone.reshape(NZ, NX, CUBE_DEV, TOPK), cube, axis=2, keepdims=False)
    mine = mine.transpose(1, 0, 2).reshape(NZ * NX, TOPK)
    owner = mine // CUBE_DEV
    return (owner % NX * NZ + owner // NX) * CUBE_DEV + mine % CUBE_DEV


def body(query_states, key_states, value_states, gate_states, selection, out_weight):
    positions = my_positions(selection)
    kv, queries = spread(query_states, key_states, value_states)
    kv = kv.reshape(2, 5 * NZ * ROWS, HEAD_DIM)
    outputs = attend(positions, kv, queries.reshape(NZ * NX, CUBE, HEAD_DIM))
    mixed = collect(outputs.reshape(NX, NZ, CUBE, HEAD_DIM))
    gates = jax.nn.sigmoid(gate_states.astype(jnp.float32))
    attended = (gates * mixed.astype(jnp.float32)).astype(jnp.bfloat16)
    return lax.psum_scatter(
        jnp.dot(attended, out_weight, preferred_element_type=jnp.float32).astype(jnp.bfloat16),
        "head",
        scatter_dimension=0,
        tiled=True,
    )


def solution(mesh):
    placed = (
        P("seq", "head"),
        P("seq", "head"),
        P("seq", "head"),
        P("seq", "head"),
        P("seq", None),
        P("head", None),
    )
    return jax.shard_map(
        body, mesh=mesh, in_specs=placed, out_specs=P(("seq", "head"), None), check_vma=False
    )
```

time: 838 us -> 229 us (0.27)
  blocking collectives: 304 us -> 37.2 us
  waiting for transfers between devices: 290 us -> 36.7 us
  Pallas kernels: 0 us -> 129 us
  local copies, waits for them, and re-layouts: 124 us -> 1.84 us
  matrix products: 47.3 us -> 8.14 us
  starting transfers between devices: 37.1 us -> 0.01 us
  other arithmetic: 18.6 us -> 0.04 us
    all_gather x2 -> x1, blocking collectives: 304 us -> 37.2 us  [my_positions(): everyone = lax.all_gather(selection, 'seq', axis=0, tiled=True)]
    all_to_all x3 -> x0, waiting for transfers between devices: 230 us -> none  [the longest x1 223 us: body(): lax.all_to_all(key_send, 'seq', split_axis=0, concat_axis=0, tiled=True)]
    pallas_call x0 -> x3, Pallas kernels: none -> 129 us  [the longest x1 78.9 us: spread(): pl.pallas_call(spread_kernel, out_shape=(jax.ShapeDtypeStruct((2, 5, NZ,...]
    reshape x6 -> x0, local copies, waits for them, and re-layouts: 73.9 us -> none  [the longest x2 70 us: arrange(): flat_tiles[slot_index].reshape(cube_dev, TOPK * CUBE, head_count, HEAD_DIM)]
    gather x6 -> x0, local copies, waits for them, and re-layouts: 44.4 us -> none  [the longest x2 27.4 us: arrange(): flat_tiles[slot_index].reshape(cube_dev, TOPK * CUBE, head_count, HEAD_DIM)]
    all_to_all x3 -> x0, starting transfers between devices: 37.1 us -> none  [the longest x1 20.1 us: body(): lax.all_to_all(value_send, 'seq', split_axis=0, concat_axis=0, tiled=True)]
    dot_general x3 -> x0, matrix products: 36.4 us -> none  [the longest x1 17.7 us: body(): jnp.einsum('chqk,ckhd->cqhd', fine_weight, arrange(got_values), preferred...]
    reduce_scatter x1, waiting for transfers between devices: 59.3 us -> 36.7 us  [body(): lax.psum_scatter(jnp.dot(attended, out_weight, preferred_element_type=jnp...]
  transfers between devices with their start and end apart: 4 -> 1, of which waited for: 3 -> 1; matrix products, arithmetic and copies ran while one was open for 12% -> 0% of each run, Pallas kernels for 0% -> 0%
where the time goes in v1:
time: 229 us; the launch traced here: 227 us
  Pallas kernels  129 us (56%)
  blocking collectives  37.2 us (16%)
  waiting for transfers between devices  36.7 us (16%)
  between operations  13.4 us (6%)
  matrix products  8.14 us (4%)
    pallas_call x1, Pallas kernels, spread(): pl.pallas_call(spread_kernel, out_shape=(jax.ShapeDtypeStruct((2, 5, NZ,...  78.9 us
    all_gather x1, blocking collectives, my_positions(): everyone = lax.all_gather(selection, 'seq', axis=0, tiled=True)  37.2 us
    reduce_scatter x1, waiting for transfers between devices, body(): lax.psum_scatter(jnp.dot(attended, out_weight, preferred_element_type=jnp...  36.7 us
    pallas_call x1, Pallas kernels, collect(): pl.pallas_call(collect_kernel, out_shape=(jax.ShapeDtypeStruct((3, 2, CUB...  30 us
    pallas_call x1, Pallas kernels, attend(): pl.pallas_call(attend_kernel, grid=(1,), out_shape=jax.ShapeDtypeStruct((...  20.3 us
    dot_general x1, matrix products, body(): jnp.dot(attended, out_weight, preferred_element_type=jnp.float32)  8.14 us
  transfers between devices with their start and end apart: 1, of which 1 were waited for; matrix products, arithmetic and copies ran while one was open for 0% of the time, Pallas kernels for 0%

profile of v1, /device:TPU:1, one launch (start us, length us, event | category | flops | bytes accessed | tf_op | source)
XLA Modules:
  0.0 226.6 jit_solution(1254814950979664284)
XLA Ops:
  6.5 0.0 copy-start.2
  6.5 0.0 reduce-scatter.2.cloned.1.call-start
  6.5 37.2 %all-gather = s32[32,6,32]{2,1,0:T(8,128)S(1)} all-gather(s32[1,6,32]{2,1,0:T(8,128)} %bitcast.48), channel_id=1, replica_groups=mesh['seq'=32,'head'=8] {'seq'}, dimensions={0}, use_global_device_ids=true | all-gather | bytes 25344 | tf_op jit(solution)/shard_map/all_gather | solution.py:393
  43.8 78.9 %spread.1 = (bf16[2,5,8,384,128]{4,3,2,1,0:T(8,128)(2,1)}, bf16[4,8,64,128]{3,2,1,0:T(8,128)(2,1)}, bf16[4,8,64,128]{3,2,1,0:T(8,128)(2,1)}) custom-call(bf16[3,2,64,640]{3,2,1,0:T(8,128)(2,1)} %bitcast.46, bf16[384,640]{1,0:T(8,128)(2,1)} %k_ref.1, bf16[384,640]{1,0:T(8,128)(2,1)} %v_ref.1), custom_call_target="tpu_custom_call" | custom-call | tf_op jit(solution)/shard_map/spread/pallas_call | solution.py:202
  122.7 0.0 copy-start.1
  122.7 1.0 copy-done.1
  123.7 20.3 %attend.1 = bf16[32,64,128]{2,1,0:T(8,128)(2,1)S(1)} custom-call(s32[32,32]{1,0:T(8,128)S(1)} %fusion.6.sel_ref, bf16[2,15360,128]{2,1,0:T(8,128)(2,1)} %bitcast.45, bf16[32,64,128]{2,1,0:T(8,128)(2,1)S(1)} %bitcast.44), custom_call_target="tpu_custom_call" | custom-call | tf_op jit(solution)/shard_map/attend/pallas_call | solution.py:372
  144.1 0.0 copy-start
  144.1 0.8 copy-done
  144.8 30.0 %collect.1 = (bf16[3,2,64,640]{3,2,1,0:T(8,128)(2,1)}, bf16[4,8,64,128]{3,2,1,0:T(8,128)(2,1)}) custom-call(bf16[4,8,64,128]{3,2,1,0:T(8,128)(2,1)} %bitcast.43), custom_call_target="tpu_custom_call" | custom-call | tf_op jit(solution)/shard_map/collect/pallas_call | solution.py:293
  174.8 0.0 copy-done.2
  174.8 8.1 %convolution_convert_fusion = bf16[384,5120]{1,0:T(8,128)(2,1)} fusion(bf16[640,5120]{1,0:T(8,128)(2,1)} %param.11, bf16[384,640]{1,0:T(8,128)(2,1)} %bitcast.49, bf16[384,640]{1,0:T(8,128)(2,1)S(1)} %copy-done.2), kind=kOutput, calls=%fused_computation | convolution fusion | flops 2520268800 | bytes 11468800 | tf_op jit(solution)/shard_map/dot_general | solution.py:411
  183.0 0.0 reduce-scatter.2.cloned.1.call-update
  183.0 36.7 %reduce-scatter.2.cloned.1.call-done = bf16[48,5120]{1,0:T(8,128)(2,1)} async-done(((bf16[384,5120]{1,0:T(8,128)(2,1)}), bf16[48,5120]{1,0:T(8,128)(2,1)}) %reduce-scatter.2.cloned.1.call-update) | async-done | bytes 491536 | tf_op jit(solution)/shard_map/reduce_scatter | solution.py:410
  (2 shorter events, 0.1 us)
Async XLA Ops:
  6.5 168.3 %copy-start.2 = (bf16[384,640]{1,0:T(8,128)(2,1)S(1)}, bf16[384,640]{1,0:T(8,128)(2,1)}, u32[]{:S(2)}) copy-start(bf16[384,640]{1,0:T(8,128)(2,1)} %param.9) | copy-start | bytes 1474564
  6.5 213.2 %reduce-scatter.2.cloned.1.call-start = ((), (), s32[]{:S(2)}) async-start(), calls=%async_computation.1 | async-start | bytes 4423680 | tf_op jit(solution)/shard_map/reduce_scatter | solution.py:410
  122.7 1.0 copy-start.1
  144.1 0.8 copy-start
Sparse Core Ops, SparseCore 0:
  183.1 36.5 reduce-scatter.1

commit v2 on v1

--- a/solution.py
+++ b/solution.py
@@ -41,7 +41,7 @@
     pltpu.make_async_copy(ref, ref, sem).wait()
 
 
-def greet(z, x, y, c):
+def greet(z, x, y, c, with_y=False):
     barrier = pltpu.get_barrier_semaphore()
     for dz in range(NZ):
         for dc in range(2):
@@ -59,12 +59,21 @@
             device_id={"seq": z * NX + (x + dx) % NX, "head": 2 * y + c},
             device_id_type=MESH,
         )
-    pl.semaphore_wait(barrier, 2 * NZ - 1 + NX - 1)
+    if with_y:
+        for dy in (1, 3):
+            pl.semaphore_signal(
+                barrier,
+                inc=1,
+                device_id={"seq": z * NX + x, "head": 2 * ((y + dy) % 4) + c},
+                device_id_type=MESH,
+            )
+    pl.semaphore_wait(barrier, 2 * NZ - 1 + NX - 1 + (2 if with_y else 0))
 
 
 def spread_kernel(
-    q_ref, k_ref, v_ref, kv_ref, qf_ref, qr_ref,
+    sel_ref, q_ref, k_ref, v_ref, kv_ref, qf_ref, all_sel_ref, qr_ref,
     z_send, z_recv, x_send, x_recv, xq_send, xq_recv, c_send, c_recv,
+    sz_send, sz_recv, sx_send, sx_recv,
 ):
     z, x, y, c = place()
     here = z * NX + x
@@ -75,6 +84,21 @@
     member = (x != 3) | has_extra
     greet(z, x, y, c)
 
+    def sel_z(n, dz):
+        return remote(
+            sel_ref, all_sel_ref.at[x, z], sz_send.at[n], sz_recv.at[z], (z + dz) % NZ * NX + x, 2 * y + c
+        )
+
+    def sel_x(dx):
+        return remote(
+            all_sel_ref.at[x], all_sel_ref.at[x], sx_send.at[dx], sx_recv.at[x], z * NX + (x + dx) % NX, 2 * y + c
+        )
+
+    pltpu.make_async_copy(sel_ref, all_sel_ref.at[x, z], sz_recv.at[z]).start()
+    for n, dz in enumerate(ORDER):
+        if dz:
+            sel_z(n, dz).start()
+
     def z_copies(act):
         for n, dz in enumerate(ORDER):
             zt = (z + dz) % NZ
@@ -111,6 +135,10 @@
                 one(is_extra, 3, q_ref.at[rank, cc, :, xcol], qr_ref.at[3, z])
 
     z_copies("start")
+    for zs in range(NZ):
+        arrived(all_sel_ref.at[x, zs], sz_recv.at[zs])
+    for dx in range(1, NX):
+        sel_x(dx).start()
 
     def x_copies(n, zs, act):
         for dx in XORDER:
@@ -189,42 +217,66 @@
                 arrived(kv_ref.at[1 - c, xs, zs], c_recv.at[xs, zs])
                 core_copy(xs, zs).wait_send()
 
+    for dx in range(1, NX):
+        arrived(all_sel_ref.at[(x + dx) % NX], sx_recv.at[(x + dx) % NX])
+        sel_x(dx).wait_send()
+    for n, dz in enumerate(ORDER):
+        if dz:
+            sel_z(n, dz).wait_send()
     z_copies("wait")
     for n, dz in enumerate(ORDER):
         x_copies(n, (z + dz) % NZ, "wait")
     xq_copies("wait")
 
 
-def spread(query_states, key_states, value_states):
+def spread(selection, query_states, key_states, value_states):
     bf16 = jnp.bfloat16
     any_spec = pl.BlockSpec(memory_space=pl.ANY)
     dma = pltpu.SemaphoreType.DMA
-    kv, qf, _ = pl.pallas_call(
+    kv, qf, all_sel, _ = pl.pallas_call(
         spread_kernel,
         out_shape=(
             jax.ShapeDtypeStruct((2, 5, NZ, ROWS, HEAD_DIM), bf16),
             jax.ShapeDtypeStruct((NX, NZ, CUBE, HEAD_DIM), bf16),
+            jax.ShapeDtypeStruct((NX, NZ, CUBE_DEV, TOPK), jnp.int32),
             jax.ShapeDtypeStruct((NX, NZ, CUBE, HEAD_DIM), bf16),
         ),
-        in_specs=[any_spec] * 3,
-        out_specs=(any_spec,) * 3,
+        in_specs=[any_spec] * 4,
+        out_specs=(any_spec,) * 4,
         scratch_shapes=[
             dma((NZ, 2, 4)), dma((NZ, 4)),
             dma((NX, NZ)), dma((NX, NZ)),
             dma((NX,)), dma((NX,)),
             dma((NX, NZ)), dma((NX, NZ)),
+            dma((NZ,)), dma((NZ,)), dma((NX,)), dma((NX,)),
         ],
         compiler_params=pltpu.CompilerParams(collective_id=0, has_side_effects=True),
         name="spread",
-    )(query_states.reshape(3, 2, CUBE, HEADS_DEV * HEAD_DIM), key_states, value_states)
-    return kv, qf
-
-
-def collect_kernel(o_ref, a_ref, relay_ref, x_send, x_recv, z_send, z_recv):
+    )(selection, query_states.reshape(3, 2, CUBE, HEADS_DEV * HEAD_DIM), key_states, value_states)
+    return kv, qf, all_sel
+
+
+NY = 4
+FEATS = HEADS_DEV * HEAD_DIM
+BAND = ROWS // NY
+BAND_CORE = BAND // 2
+COLS = 2560
+TILE = 640
+TILES = COLS // TILE
+
+
+def finish_kernel(
+    o_ref, gate_ref, w_ref, out_ref,
+    relay_ref, a_ref, att, weight, part, passed, landed, done,
+    x_send, x_recv, z_send, z_recv, w_sem, t_sem,
+    part_send, passed_recv, landed_recv, done_send, done_recv,
+):
+    f32, bf16 = jnp.float32, jnp.bfloat16
     z, x, y, c = place()
+    here = z * NX + x
     has_extra = z % 4 != 3
     member = (x != 3) | has_extra
-    greet(z, x, y, c)
+    greet(z, x, y, c, True)
 
     def x_copies(act):
         for dx in range(NX):
@@ -241,6 +293,20 @@
                 pltpu.make_async_copy(o_ref.at[x], relay_ref.at[x], x_recv.at[x]).start()
 
     pl.when(member)(lambda: x_copies("start"))
+
+    def half(core):
+        return pl.ds(pl.multiple_of(core * COLS, COLS), COLS)
+
+    def block(core):
+        return pl.ds(pl.multiple_of(core * FEATS, FEATS), FEATS)
+
+    w_own = pltpu.make_async_copy(w_ref.at[:, half(c)], weight.at[block(c)], w_sem.at[0])
+    w_away = remote(
+        w_ref.at[:, half(1 - c)], weight.at[block(c)], w_sem.at[1], w_sem.at[2], here, 2 * y + 1 - c
+    )
+    w_own.start()
+    w_away.start()
+
     for xs in range(3):
         arrived(relay_ref.at[xs], x_recv.at[xs])
     pl.when(has_extra)(lambda: arrived(relay_ref.at[3], x_recv.at[3]))
@@ -282,27 +348,110 @@
             if zs % 4 != 3:
                 xcol = pl.ds((3 + zs // 4) * HEAD_DIM, HEAD_DIM)
                 pl.when(c == 1)(lambda: arrived(a_ref.at[zs % 4, cc, :, xcol], z_recv.at[zs, cc, 1]))
+
+    mixed = a_ref[...].reshape(ROWS, FEATS).astype(f32)
+    att[c] = (jax.nn.sigmoid(gate_ref[...].astype(f32)) * mixed).astype(bf16)
+    att_away = remote(att.at[c], att.at[c], t_sem.at[0], t_sem.at[1], here, 2 * y + 1 - c)
+    att_away.start()
+    w_own.wait()
+    arrived(weight.at[block(1 - c)], w_sem.at[2])
+    arrived(att.at[1 - c], t_sem.at[1])
+
+    def product(band, t):
+        rows = pl.ds(pl.multiple_of(band * BAND, BAND), BAND)
+        cols = slice(t * TILE, (t + 1) * TILE)
+        total = jnp.dot(att[0, rows, :], weight[:FEATS, cols], preferred_element_type=f32)
+        return total + jnp.dot(att[1, rows, :], weight[FEATS:, cols], preferred_element_type=f32)
+
+    right, left = (y + 1) % NY, (y + 3) % NY
+
+    def across(t):
+        return remote(
+            part.at[1, t], passed.at[t], part_send.at[1, t], passed_recv.at[t],
+            here, 2 * (right if t < 2 else left) + c,
+        )
+
+    def onward(side, t):
+        return remote(
+            part.at[2 * side, t], landed.at[side, t], part_send.at[2 * side, t], landed_recv.at[side, t],
+            here, 2 * (left if side else right) + c,
+        )
+
+    for t in (0, 2, 1, 3):
+        part[1, t] = product((y + 2) % NY, t).astype(bf16)
+        across(t).start()
+    for side, t in ((0, 2), (1, 0), (0, 3), (1, 1)):
+        part[2 * side, t] = product(left if side else right, t).astype(bf16)
+        onward(side, t).start()
+    for side, t in ((0, 0), (1, 2), (0, 1), (1, 3)):
+        total = product(left if side else right, t)
+        arrived(passed.at[t], passed_recv.at[t])
+        part[2 * side, t] = (total + passed[t].astype(f32)).astype(bf16)
+        onward(side, t).start()
+
+    def rows_of(core):
+        return pl.ds(pl.multiple_of(core * BAND_CORE, BAND_CORE), BAND_CORE)
+
+    def columns(core, t):
+        return pl.ds(pl.multiple_of(core * COLS + t * TILE, TILE), TILE)
+
+    def give(t):
+        return remote(
+            done.at[t, rows_of(1 - c)], out_ref.at[:, columns(c, t)],
+            done_send.at[0, t], done_recv.at[t], here, 2 * y + 1 - c,
+        )
+
+    def keep(t):
+        return pltpu.make_async_copy(done.at[t, rows_of(c)], out_ref.at[:, columns(c, t)], done_send.at[1, t])
+
+    for t in (2, 0, 3, 1):
+        total = product(y, t)
+        for side in range(2):
+            arrived(landed.at[side, t], landed_recv.at[side, t])
+            total = total + landed[side, t].astype(f32)
+        done[t] = total.astype(bf16)
+        give(t).start()
+        keep(t).start()
+
+    for t in range(TILES):
+        give(t).wait_send()
+        keep(t).wait()
+        arrived(out_ref.at[:, columns(1 - c, t)], done_recv.at[t])
+        across(t).wait_send()
+        for side in range(2):
+            onward(side, t).wait_send()
+    w_away.wait_send()
+    att_away.wait_send()
     pl.when(member)(lambda: x_copies("wait"))
     z_copies("wait")
 
 
-def collect(outputs):
+def finish(outputs, gate_states, out_weight):
     bf16 = jnp.bfloat16
     any_spec = pl.BlockSpec(memory_space=pl.ANY)
-    dma = pltpu.SemaphoreType.DMA
-    attended, _ = pl.pallas_call(
-        collect_kernel,
-        out_shape=(
-            jax.ShapeDtypeStruct((3, 2, CUBE, HEADS_DEV * HEAD_DIM), bf16),
-            jax.ShapeDtypeStruct((NX, NZ, CUBE, HEAD_DIM), bf16),
+    dma, vmem = pltpu.SemaphoreType.DMA, pltpu.VMEM
+    return pl.pallas_call(
+        finish_kernel,
+        out_shape=jax.ShapeDtypeStruct((BAND_CORE, 2 * COLS), bf16),
+        in_specs=[any_spec, pl.BlockSpec(memory_space=pltpu.VMEM), any_spec],
+        out_specs=any_spec,
+        scratch_shapes=[
+            vmem((NX, NZ, CUBE, HEAD_DIM), bf16),
+            vmem((3, 2, CUBE, FEATS), bf16),
+            vmem((2, ROWS, FEATS), bf16),
+            vmem((2 * FEATS, COLS), bf16),
+            vmem((3, TILES, BAND, TILE), bf16),
+            vmem((TILES, BAND, TILE), bf16),
+            vmem((2, TILES, BAND, TILE), bf16),
+            vmem((TILES, BAND, TILE), bf16),
+            dma((NX,)), dma((NX,)), dma((NZ, 2)), dma((NZ, 2, 2)), dma((3,)), dma((2,)),
+            dma((3, TILES)), dma((TILES,)), dma((2, TILES)), dma((2, TILES)), dma((TILES,)),
+        ],
+        compiler_params=pltpu.CompilerParams(
+            collective_id=1, has_side_effects=True, vmem_limit_bytes=40 * 2**20
         ),
-        in_specs=[any_spec],
-        out_specs=(any_spec,) * 2,
-        scratch_shapes=[dma((NX,)), dma((NX,)), dma((NZ, 2)), dma((NZ, 2, 2))],
-        compiler_params=pltpu.CompilerParams(collective_id=1, has_side_effects=True),
-        name="collect",
-    )(outputs)
-    return attended.reshape(ROWS, HEADS_DEV * HEAD_DIM)
+        name="finish",
+    )(outputs, gate_states, out_weight)
 
 
 CONTRACT_LAST = (((1,), (1,)), ((), ()))
@@ -388,31 +537,20 @@
     )(positions, kv, queries)
 
 
-def my_positions(selection):
+def my_positions(all_sel):
     z, x, _, c = place()
-    everyone = lax.all_gather(selection, "seq", axis=0, tiled=True)
     rank = x + x // 3 * (z % 4 - x)
     cube = jnp.minimum(2 * rank + c, CUBE_DEV - 1)
-    mine = lax.dynamic_index_in_dim(everyone.reshape(NZ, NX, CUBE_DEV, TOPK), cube, axis=2, keepdims=False)
-    mine = mine.transpose(1, 0, 2).reshape(NZ * NX, TOPK)
+    mine = lax.dynamic_index_in_dim(all_sel, cube, axis=2, keepdims=False).reshape(NZ * NX, TOPK)
     owner = mine // CUBE_DEV
     return (owner % NX * NZ + owner // NX) * CUBE_DEV + mine % CUBE_DEV
 
 
 def body(query_states, key_states, value_states, gate_states, selection, out_weight):
-    positions = my_positions(selection)
-    kv, queries = spread(query_states, key_states, value_states)
+    kv, queries, all_sel = spread(selection, query_states, key_states, value_states)
     kv = kv.reshape(2, 5 * NZ * ROWS, HEAD_DIM)
-    outputs = attend(positions, kv, queries.reshape(NZ * NX, CUBE, HEAD_DIM))
-    mixed = collect(outputs.reshape(NX, NZ, CUBE, HEAD_DIM))
-    gates = jax.nn.sigmoid(gate_states.astype(jnp.float32))
-    attended = (gates * mixed.astype(jnp.float32)).astype(jnp.bfloat16)
-    return lax.psum_scatter(
-        jnp.dot(attended, out_weight, preferred_element_type=jnp.float32).astype(jnp.bfloat16),
-        "head",
-        scatter_dimension=0,
-        tiled=True,
-    )
+    outputs = attend(my_positions(all_sel), kv, queries.reshape(NZ * NX, CUBE, HEAD_DIM))
+    return finish(outputs.reshape(NX, NZ, CUBE, HEAD_DIM), gate_states, out_weight)
 
 
 def solution(mesh):

time: 229 us -> 151 us (0.66); the launches traced: 227 us -> 151 us
  blocking collectives: 37.2 us -> 0 us
  waiting for transfers between devices: 36.7 us -> 0 us
  Pallas kernels: 129 us -> 147 us
  between operations: 13.4 us -> 0.14 us
  matrix products: 8.14 us -> 0 us
  other arithmetic: 0.04 us -> 2.36 us
    all_gather x1 -> x0, blocking collectives: 37.2 us -> none  [my_positions(): everyone = lax.all_gather(selection, 'seq', axis=0, tiled=True)]
    reduce_scatter x1 -> x0, waiting for transfers between devices: 36.7 us -> none  [body(): lax.psum_scatter(jnp.dot(attended, out_weight, preferred_element_type=jnp...]
    pallas_call x1, Pallas kernels: 30 us -> 51.5 us  [finish(): pl.pallas_call(finish_kernel, out_shape=jax.ShapeDtypeStruct((BAND_CORE,...]
    dot_general x1 -> x0, matrix products: 8.14 us -> none  [body(): jnp.dot(attended, out_weight, preferred_element_type=jnp.float32)]
    pallas_call x1, Pallas kernels: 78.9 us -> 75.1 us  [spread(): pl.pallas_call(spread_kernel, out_shape=(jax.ShapeDtypeStruct((2, 5, NZ,...]
  transfers between devices with their start and end apart: 1 -> 0, of which waited for: 1 -> 0; matrix products, arithmetic and copies ran while one was open for 0% -> 0% of each run, Pallas kernels for 0% -> 0%
where the time goes in v2:
time: 151 us
  Pallas kernels  147 us (97%)
  other arithmetic  2.36 us (2%)
  local copies, waits for them, and re-layouts  1.83 us (1%)
    pallas_call x1, Pallas kernels, spread(): pl.pallas_call(spread_kernel, out_shape=(jax.ShapeDtypeStruct((2, 5, NZ,...  75.1 us
    pallas_call x1, Pallas kernels, finish(): pl.pallas_call(finish_kernel, out_shape=jax.ShapeDtypeStruct((BAND_CORE,...  51.5 us
    pallas_call x1, Pallas kernels, attend(): pl.pallas_call(attend_kernel, grid=(1,), out_shape=jax.ShapeDtypeStruct((...  20.3 us

profile of v2, /device:TPU:1, one launch (start us, length us, event | category | flops | bytes accessed | tf_op | source)
XLA Modules:
  0.0 151.2 jit_solution(1110965621569198459)
XLA Ops:
  0.0 0.0 copy-start.2
  0.0 75.1 %spread.1 = (bf16[2,5,8,384,128]{4,3,2,1,0:T(8,128)(2,1)}, bf16[4,8,64,128]{3,2,1,0:T(8,128)(2,1)}, s32[4,8,6,32]{3,2,1,0:T(8,128)}, bf16[4,8,64,128]{3,2,1,0:T(8,128)(2,1)}) custom-call(s32[6,32]{1,0:T(8,128)} %sel_ref.1, bf16[3,2,64,640]{3,2,1,0:T(8,128)(2,1)} %bitcast.13, bf16[384,640]{1,0:T(8,128)(2,1)} %k_ref.1, bf16[384,640]{1,0:T(8,128)(2,1)} %v_ref.1), custom_call_target="tpu_custom_call" | custom-call | tf_op jit(solution)/shard_map/spread/pallas_call | solution.py:236
  75.2 0.0 copy-start
  75.2 1.1 broadcast_divide_fusion
  76.3 1.2 sign_compare_fusion.1
  77.6 0.0 copy-start.1
  77.6 1.0 copy-done.1
  78.6 20.3 %attend.1 = bf16[32,64,128]{2,1,0:T(8,128)(2,1)S(1)} custom-call(s32[32,32]{1,0:T(8,128)S(1)} %fusion.3.sel_ref, bf16[2,15360,128]{2,1,0:T(8,128)(2,1)} %bitcast.12, bf16[32,64,128]{2,1,0:T(8,128)(2,1)S(1)} %bitcast.11), custom_call_target="tpu_custom_call" | custom-call | tf_op jit(solution)/shard_map/attend/pallas_call | solution.py:521
  98.9 0.0 copy-done.2
  99.0 0.0 copy-done
  99.0 51.5 %finish.1 = bf16[48,5120]{1,0:T(8,128)(2,1)S(1)} custom-call(bf16[4,8,64,128]{3,2,1,0:T(8,128)(2,1)S(1)} %bitcast.10, bf16[384,640]{1,0:T(8,128)(2,1)S(1)} %copy-done.2, bf16[640,5120]{1,0:T(8,128)(2,1)S(1)} %copy-done), custom_call_target="tpu_custom_call" | custom-call | tf_op jit(solution)/shard_map/finish/pallas_call | solution.py:433
  150.5 0.8 copy.10
  (1 shorter events, 0.0 us)
Async XLA Ops:
  0.0 99.0 %copy-start.2 = (bf16[384,640]{1,0:T(8,128)(2,1)S(1)}, bf16[384,640]{1,0:T(8,128)(2,1)}, u32[]{:S(2)}) copy-start(bf16[384,640]{1,0:T(8,128)(2,1)} %gate_ref.1) | copy-start | bytes 1474564
  75.2 23.8 %copy-start = (bf16[640,5120]{1,0:T(8,128)(2,1)S(1)}, bf16[640,5120]{1,0:T(8,128)(2,1)}, u32[]{:S(2)}) copy-start(bf16[640,5120]{1,0:T(8,128)(2,1)} %w_ref.1) | copy-start | bytes 19660804
  77.6 1.0 copy-start.1

commit v3 on v2

v3 whole, which is shorter than its diff:
```python
import functools
import math

import jax
import jax.numpy as jnp
from jax import lax
from jax.experimental import pallas as pl
from jax.experimental.pallas import tpu as pltpu
from jax.sharding import PartitionSpec as P

MESH = pl.DeviceIdType.MESH
HEAD_DIM = 128
CUBE = 64
CUBE_DEV = 6
TOPK = 32
NZ, NX = 8, 4
ROWS = CUBE * CUBE_DEV
HEADS_DEV = 5
NY = 4
ORDER = (0, 1, 7, 2, 6, 3, 5, 4)
XORDER = (1, 3, 2)
FEATS = HEADS_DEV * HEAD_DIM
BAND = ROWS // NY
BAND_CORE = BAND // 2
COLS = 2560
TILE = 640
TILES = COLS // TILE
N_CUBES = NZ * NX * CUBE_DEV
GROUP = 4
WIDTH = GROUP * CUBE
LAG = 2
CONTRACT_LAST = (((1,), (1,)), ((), ()))
EXP_SCALE = HEAD_DIM ** (-0.5) * math.log2(math.e)


def place():
    seq, head = lax.axis_index("seq"), lax.axis_index("head")
    return seq // NX, seq % NX, head // 2, head % 2


def remote(src, dst, send_sem, recv_sem, seq, head):
    return pltpu.make_async_remote_copy(
        src_ref=src,
        dst_ref=dst,
        send_sem=send_sem,
        recv_sem=recv_sem,
        device_id={"seq": seq, "head": head},
        device_id_type=MESH,
    )


def arrived(ref, sem):
    pltpu.make_async_copy(ref, ref, sem).wait()


def greet(z, x, y, c):
    barrier = pltpu.get_barrier_semaphore()
    for dz in range(NZ):
        for dc in range(2):
            if dz or dc:
                pl.semaphore_signal(
                    barrier,
                    inc=1,
                    device_id={"seq": (z + dz) % NZ * NX + x, "head": 2 * y + (c + dc) % 2},
                    device_id_type=MESH,
                )
    for dx in range(1, NX):
        pl.semaphore_signal(
            barrier,
            inc=1,
            device_id={"seq": z * NX + (x + dx) % NX, "head": 2 * y + c},
            device_id_type=MESH,
        )
    for dy in (1, 3):
        pl.semaphore_signal(
            barrier,
            inc=1,
            device_id={"seq": z * NX + x, "head": 2 * ((y + dy) % NY) + c},
            device_id_type=MESH,
        )
    pl.semaphore_wait(barrier, 2 * NZ - 1 + NX - 1 + 2)


def kernel(
    sel_ref, q_ref, k_ref, v_ref, gate_ref, w_ref, out_ref,
    kv_ref, qr_ref, qf_ref, all_sel_ref, sel, pooled, scores, o_ref,
    relay_ref, a_ref, att, weight, part, passed, landed, done,
    z_send, z_recv, x_send, x_recv, xq_send, xq_recv, c_send, c_recv,
    sz_send, sz_recv, sx_send, sx_recv, pick_sem,
    o_send, o_recv, r_send, r_recv, w_sem, t_sem,
    part_send, passed_recv, landed_recv, done_send, done_recv,
):
    f32, bf16 = jnp.float32, jnp.bfloat16
    z, x, y, c = place()
    here = z * NX + x
    sibling = 2 * y + 1 - c
    main_slot = x + x // 3
    extra_slot = 4 - x // 3
    has_extra = z % 4 != 3
    member = (x != 3) | has_extra
    greet(z, x, y, c)

    def tile_at(which, slot, zs):
        return kv_ref.at[which, pl.ds((slot * NZ + zs) * CUBE_DEV, CUBE_DEV)]

    def half(core):
        return pl.ds(pl.multiple_of(core * COLS, COLS), COLS)

    def block(core):
        return pl.ds(pl.multiple_of(core * FEATS, FEATS), FEATS)

    w_own = pltpu.make_async_copy(w_ref.at[:, half(c)], weight.at[block(c)], w_sem.at[0])
    w_away = remote(w_ref.at[:, half(1 - c)], weight.at[block(c)], w_sem.at[1], w_sem.at[2], here, sibling)

    def sel_z(n, dz):
        return remote(
            sel_ref, all_sel_ref.at[x, z], sz_send.at[n], sz_recv.at[z], (z + dz) % NZ * NX + x, 2 * y + c
        )

    def sel_x(dx):
        return remote(
            all_sel_ref.at[x], all_sel_ref.at[x], sx_send.at[dx], sx_recv.at[x], z * NX + (x + dx) % NX, 2 * y + c
        )

    pltpu.make_async_copy(sel_ref, all_sel_ref.at[x, z], sz_recv.at[z]).start()
    for n, dz in enumerate(ORDER):
        if dz:
            sel_z(n, dz).start()

    def z_copies(act):
        for n, dz in enumerate(ORDER):
            zt = (z + dz) % NZ
            for cc in range(2):
                source = k_ref if cc == 0 else v_ref

                def one(cond, kind, src, dst):
                    def away():
                        copy = remote(
                            src, dst, z_send.at[n, cc, kind], z_recv.at[z, kind], zt * NX + x, 2 * y + cc
                        )
                        if act == "start":
                            copy.start()
                        else:
                            copy.wait_send()

                    if dz:
                        pl.when(cond)(away)
                    else:
                        pl.when(cond & (c != cc))(away)
                        if act == "start":
                            pl.when(cond & (c == cc))(
                                lambda: pltpu.make_async_copy(src, dst, z_recv.at[z, kind]).start()
                            )

                is_main = c == zt // 5
                col = pl.ds(pl.multiple_of(zt % 5 * HEAD_DIM, HEAD_DIM), HEAD_DIM)
                one(is_main, 0, source.at[:, :, col], tile_at(cc, main_slot, z))
                is_extra = (c == 1) & (zt % 4 != 3)
                xcol = pl.ds(pl.multiple_of((3 + zt // 4) * HEAD_DIM, HEAD_DIM), HEAD_DIM)
                one(is_extra, 1, source.at[:, :, xcol], tile_at(cc, extra_slot, z))
                one(is_main, 2, q_ref.at[:, cc, :, col], qr_ref.at[pl.ds(0, 3), z])
                rank = zt % 4 - zt % 4 // 3
                one(is_extra, 3, q_ref.at[rank, cc, :, xcol], qr_ref.at[3, z])

    z_copies("start")
    w_own.start()
    w_away.start()
    for zs in range(NZ):
        arrived(all_sel_ref.at[x, zs], sz_recv.at[zs])
    for dx in range(1, NX):
        sel_x(dx).start()

    def x_copies(n, zs, act):
        for dx in XORDER:
            xt = (x + dx) % NX
            slot = main_slot + xt // 3 * (4 - main_slot)

            def away():
                copy = remote(
                    tile_at(c, slot, zs), tile_at(c, x, zs),
                    x_send.at[dx, n], x_recv.at[x, zs], z * NX + xt, 2 * y + c,
                )
                if act == "start":
                    copy.start()
                else:
                    copy.wait_send()

            pl.when((xt != 3) | has_extra)(away)

    def core_copy(xs, zs):
        return remote(
            tile_at(c, xs, zs), tile_at(c, xs, zs),
            c_send.at[xs, zs], c_recv.at[xs, zs], here, sibling,
        )

    def take_x(zs):
        for dx in XORDER:
            xs = (x + dx) % NX

            @pl.when(member)
            def _():
                arrived(tile_at(c, xs, zs), x_recv.at[xs, zs])
                core_copy(xs, zs).start()

    for n, dz in enumerate(ORDER):
        zs = (z + dz) % NZ
        arrived(tile_at(c, main_slot, zs), z_recv.at[zs, 0])
        pl.when(has_extra)(lambda: arrived(tile_at(c, extra_slot, zs), z_recv.at[zs, 1]))
        x_copies(n, zs, "start")
        pl.when(member)(lambda: core_copy(x, zs).start())
        if n >= LAG:
            take_x((z + ORDER[n - LAG]) % NZ)

    for zs in range(NZ):
        arrived(qr_ref.at[pl.ds(0, 3), zs], z_recv.at[zs, 2])
        pl.when(has_extra)(lambda: arrived(qr_ref.at[3, zs], z_recv.at[zs, 3]))

    def xq_copies(act):
        for dx in range(NX):
            xt = (x + dx) % NX

            def away():
                if dx:
                    copy = remote(
                        qr_ref.at[xt], qf_ref.at[x], xq_send.at[dx], xq_recv.at[x], z * NX + xt, 2 * y + c
                    )
                    if act == "start":
                        copy.start()
                    else:
                        copy.wait_send()
                elif act == "start":
                    pltpu.make_async_copy(qr_ref.at[x], qf_ref.at[x], xq_recv.at[x]).start()

            pl.when((xt != 3) | has_extra)(away)

    xq_copies("start")
    for n in range(NZ - LAG, NZ):
        take_x((z + ORDER[n]) % NZ)

    for dx in range(1, NX):
        arrived(all_sel_ref.at[(x + dx) % NX], sx_recv.at[(x + dx) % NX])
    picks = pltpu.make_async_copy(all_sel_ref, sel, pick_sem)
    picks.start()

    @pl.when(member)
    def _():
        for xs in range(NX):
            arrived(qf_ref.at[xs], xq_recv.at[xs])
        for xs in range(NX):
            for zs in range(NZ):
                arrived(tile_at(1 - c, xs, zs), c_recv.at[xs, zs])

    picks.wait()

    rank = x + x // 3 * (z % 4 - x)
    cube = rank * 2 + c - rank // 3 * 2

    def pool(i, _):
        for which in range(2):
            block_of = kv_ref[which, pl.ds(i * 16, 16)].astype(f32)
            sums = jnp.sum(block_of, axis=1)
            pooled[which, pl.ds(pl.multiple_of(i * 16, 16), 16), :] = (sums * (1.0 / CUBE)).astype(bf16)
        return 0

    lax.fori_loop(0, N_CUBES // 16, pool, 0)

    def target(n):
        return (z + 4 + (1 - n % 2 * 2) * ((n + 1) // 2)) % NZ

    def rows(which, xs, zs, g):
        tiles = [
            kv_ref[which, sel[xs, zs, cube, g * GROUP + n]]
            for n in range(GROUP)
        ]
        return jnp.concatenate(tiles, axis=0)

    def pair_rows(which, pair, zs, g):
        return jnp.concatenate([rows(which, 2 * pair, zs, g), rows(which, 2 * pair + 1, zs, g)], axis=1)

    def blend(pair, zs, top, pair_ahead, zs_ahead):
        acc = [jnp.zeros((CUBE, HEAD_DIM), f32) for _ in range(2)]
        total = jnp.zeros((2 * CUBE, 128), f32)
        peak = None
        if top is not None:
            q = jnp.concatenate([qf_ref[2 * pair, zs], qf_ref[2 * pair + 1, zs]], axis=0)
            s = lax.dot_general(q, pooled[0], CONTRACT_LAST, preferred_element_type=f32)
            e = jnp.exp2((s - jnp.max(s, axis=1, keepdims=True)) * EXP_SCALE)
            coarse = jnp.dot(e.astype(bf16), pooled[1], preferred_element_type=f32)
            coarse = coarse / jnp.sum(e, axis=1, keepdims=True)
        zero = jnp.zeros((CUBE, HEAD_DIM), bf16)
        ahead = jnp.concatenate([
            jnp.concatenate([qf_ref[2 * pair_ahead, zs_ahead], zero], axis=1),
            jnp.concatenate([zero, qf_ref[2 * pair_ahead + 1, zs_ahead]], axis=1),
        ], axis=0)
        for g in range(TOPK // GROUP):
            cols = slice(g * WIDTH, (g + 1) * WIDTH)
            s = lax.dot_general(ahead, pair_rows(0, pair_ahead, zs_ahead, g), CONTRACT_LAST, preferred_element_type=f32)
            scores[pair_ahead, :, cols] = s
            part_peak = jnp.maximum(s[:, :128], s[:, 128:])
            peak = part_peak if peak is None else jnp.maximum(peak, part_peak)
            if top is not None:
                e = jnp.exp2((scores[pair, :, cols] - top) * EXP_SCALE)
                total = total + (e[:, :128] + e[:, 128:])
                out = jnp.dot(e.astype(bf16), pair_rows(1, pair, zs, g), preferred_element_type=f32)
                acc = [acc[0] + out[:CUBE, :HEAD_DIM], acc[1] + out[CUBE:, HEAD_DIM:]]
        if top is not None:
            mixed = jnp.concatenate(acc, axis=0) / jnp.sum(total, axis=1, keepdims=True) + coarse
            for n in range(2):
                o_ref[2 * pair + n, zs] = mixed[n * CUBE:(n + 1) * CUBE].astype(bf16)
        return jnp.max(peak, axis=1, keepdims=True)

    def o_copy(dx, n, zs):
        xt = (x + dx) % NX
        return remote(
            o_ref.at[xt, zs], relay_ref.at[x, zs], o_send.at[dx, n], o_recv.at[x, zs], z * NX + xt, 2 * y + c
        )

    def pass_copies(n, zs, act):
        def one(cond, kind, core, src, dst):
            def away():
                copy = remote(src, dst, r_send.at[n, kind], r_recv.at[z, c, kind], zs * NX + x, 2 * y + core)
                if act == "start":
                    copy.start()
                else:
                    copy.wait_send()

            stays = (zs == z) & (c == core)
            pl.when(cond & jnp.logical_not(stays))(away)
            if act == "start":
                pl.when(cond & stays)(
                    lambda: pltpu.make_async_copy(src, dst, r_recv.at[z, c, kind]).start()
                )

        col = pl.ds(pl.multiple_of(z % 5 * HEAD_DIM, HEAD_DIM), HEAD_DIM)
        one(z >= 0, 0, z // 5, relay_ref.at[pl.ds(0, 3), zs], a_ref.at[:, c, :, col])
        xcol = pl.ds(pl.multiple_of((3 + z // 4) * HEAD_DIM, HEAD_DIM), HEAD_DIM)
        third = z % 4 - z % 4 // 3
        one(has_extra, 1, 1, relay_ref.at[3, zs], a_ref.at[third, c, :, xcol])

    def pass_on(n):
        zs = target(n)
        for xs in range(3):
            arrived(relay_ref.at[xs, zs], o_recv.at[xs, zs])
        pl.when(has_extra)(lambda: arrived(relay_ref.at[3, zs], o_recv.at[3, zs]))
        pass_copies(n, zs, "start")

    def step(n, top):
        zs = target(n)
        top = blend(0, zs, top, 1, zs)
        top = blend(1, zs, top, 0, target(jnp.minimum(n + 1, NZ - 1)))

        @pl.when(member)
        def _():
            pltpu.make_async_copy(o_ref.at[x, zs], relay_ref.at[x, zs], o_recv.at[x, zs]).start()
            for dx in XORDER:
                o_copy(dx, n, zs).start()

        pl.when(n >= LAG)(lambda: pass_on(n - LAG))
        return top

    lax.fori_loop(0, NZ, step, blend(None, None, None, 0, target(0)))
    for n in range(NZ - LAG, NZ):
        pass_on(n)

    for zs in range(NZ):
        for cc in range(2):
            col = pl.ds(zs % 5 * HEAD_DIM, HEAD_DIM)
            pl.when(c == zs // 5)(lambda: arrived(a_ref.at[:, cc, :, col], r_recv.at[zs, cc, 0]))
            if zs % 4 != 3:
                xcol = pl.ds((3 + zs // 4) * HEAD_DIM, HEAD_DIM)
                pl.when(c == 1)(lambda: arrived(a_ref.at[zs % 4, cc, :, xcol], r_recv.at[zs, cc, 1]))

    mixed = a_ref[...].reshape(ROWS, FEATS).astype(f32)
    att[c] = (jax.nn.sigmoid(gate_ref[...].astype(f32)) * mixed).astype(bf16)
    att_away = remote(att.at[c], att.at[c], t_sem.at[0], t_sem.at[1], here, sibling)
    att_away.start()
    w_own.wait()
    arrived(weight.at[block(1 - c)], w_sem.at[2])
    arrived(att.at[1 - c], t_sem.at[1])

    def product(band, t):
        rows = pl.ds(pl.multiple_of(band * BAND, BAND), BAND)
        cols = slice(t * TILE, (t + 1) * TILE)
        total = jnp.dot(att[0, rows, :], weight[:FEATS, cols], preferred_element_type=f32)
        return total + jnp.dot(att[1, rows, :], weight[FEATS:, cols], preferred_element_type=f32)

    right, left = (y + 1) % NY, (y + 3) % NY

    def across(t):
        return remote(
            part.at[1, t], passed.at[t], part_send.at[1, t], passed_recv.at[t],
            here, 2 * (right if t < 2 else left) + c,
        )

    def onward(side, t):
        return remote(
            part.at[2 * side, t], landed.at[side, t], part_send.at[2 * side, t], landed_recv.at[side, t],
            here, 2 * (left if side else right) + c,
        )

    for t in (0, 2, 1, 3):
        part[1, t] = product((y + 2) % NY, t).astype(bf16)
        across(t).start()
    for side, t in ((0, 2), (1, 0), (0, 3), (1, 1)):
        part[2 * side, t] = product(left if side else right, t).astype(bf16)
        onward(side, t).start()
    for side, t in ((0, 0), (1, 2), (0, 1), (1, 3)):
        total = product(left if side else right, t)
        arrived(passed.at[t], passed_recv.at[t])
        part[2 * side, t] = (total + passed[t].astype(f32)).astype(bf16)
        onward(side, t).start()

    def rows_of(core):
        return pl.ds(pl.multiple_of(core * BAND_CORE, BAND_CORE), BAND_CORE)

    def columns(core, t):
        return pl.ds(pl.multiple_of(core * COLS + t * TILE, TILE), TILE)

    def give(t):
        return remote(
            done.at[t, rows_of(1 - c)], out_ref.at[:, columns(c, t)],
            done_send.at[0, t], done_recv.at[t], here, 2 * y + 1 - c,
        )

    def keep(t):
        return pltpu.make_async_copy(done.at[t, rows_of(c)], out_ref.at[:, columns(c, t)], done_send.at[1, t])

    for t in (2, 0, 3, 1):
        total = product(y, t)
        for side in range(2):
            arrived(landed.at[side, t], landed_recv.at[side, t])
            total = total + landed[side, t].astype(f32)
        done[t] = total.astype(bf16)
        give(t).start()
        keep(t).start()

    for t in range(TILES):
        give(t).wait_send()
        keep(t).wait()
        arrived(out_ref.at[:, columns(1 - c, t)], done_recv.at[t])
        across(t).wait_send()
        for side in range(2):
            onward(side, t).wait_send()
    w_away.wait_send()
    att_away.wait_send()

    @pl.when(member)
    def _():
        for n in range(NZ):
            for dx in XORDER:
                o_copy(dx, n, target(n)).wait_send()
        for xs in range(NX):
            for zs in range(NZ):
                core_copy(xs, zs).wait_send()

    for n in range(NZ):
        pass_copies(n, target(n), "wait")
    for dx in range(1, NX):
        sel_x(dx).wait_send()
    for n, dz in enumerate(ORDER):
        if dz:
            sel_z(n, dz).wait_send()
    z_copies("wait")
    for n, dz in enumerate(ORDER):
        x_copies(n, (z + dz) % NZ, "wait")
    xq_copies("wait")


def body(query_states, key_states, value_states, gate_states, selection, out_weight):
    bf16 = jnp.bfloat16
    any_spec = pl.BlockSpec(memory_space=pl.ANY)
    dma, vmem = pltpu.SemaphoreType.DMA, pltpu.VMEM
    owner = selection // CUBE_DEV
    places = (owner % NX * NZ + owner // NX) * CUBE_DEV + selection % CUBE_DEV
    places = jnp.pad(places, ((0, 8 - CUBE_DEV), (0, 128 - TOPK)))
    cubes = vmem((NX, NZ, CUBE, HEAD_DIM), bf16)
    return pl.pallas_call(
        kernel,
        out_shape=jax.ShapeDtypeStruct((BAND_CORE, 2 * COLS), bf16),
        in_specs=[any_spec] * 4 + [pl.BlockSpec(memory_space=pltpu.VMEM), any_spec],
        out_specs=any_spec,
        scratch_shapes=[
            vmem((2, 5 * NZ * CUBE_DEV, CUBE, HEAD_DIM), bf16),
            cubes,
            cubes,
            vmem((NX, NZ, 8, 128), jnp.int32),
            pltpu.SMEM((NX, NZ, 8, 128), jnp.int32),
            vmem((2, N_CUBES, HEAD_DIM), bf16),
            vmem((2, 2 * CUBE, TOPK * CUBE), jnp.float32),
            cubes,
            cubes,
            vmem((3, 2, CUBE, FEATS), bf16),
            vmem((2, ROWS, FEATS), bf16),
            vmem((2 * FEATS, COLS), bf16),
            vmem((3, TILES, BAND, TILE), bf16),
            vmem((TILES, BAND, TILE), bf16),
            vmem((2, TILES, BAND, TILE), bf16),
            vmem((TILES, BAND, TILE), bf16),
            dma((NZ, 2, 4)), dma((NZ, 4)),
            dma((NX, NZ)), dma((NX, NZ)),
            dma((NX,)), dma((NX,)),
            dma((NX, NZ)), dma((NX, NZ)),
            dma((NZ,)), dma((NZ,)), dma((NX,)), dma((NX,)), dma,
            dma((NX, NZ)), dma((NX, NZ)), dma((NZ, 2)), dma((NZ, 2, 2)), dma((3,)), dma((2,)),
            dma((3, TILES)), dma((TILES,)), dma((2, TILES)), dma((2, TILES)), dma((TILES,)),
        ],
        compiler_params=pltpu.CompilerParams(
            collective_id=0, has_side_effects=True, vmem_limit_bytes=48 * 2**20
        ),
        name="sparse_attention",
    )(
        places,
        query_states.reshape(3, 2, CUBE, FEATS),
        key_states.reshape(CUBE_DEV, CUBE, FEATS),
        value_states.reshape(CUBE_DEV, CUBE, FEATS),
        gate_states,
        out_weight,
    )


def solution(mesh):
    placed = (
        P("seq", "head"),
        P("seq", "head"),
        P("seq", "head"),
        P("seq", "head"),
        P("seq", None),
        P("head", None),
    )
    return jax.shard_map(
        body, mesh=mesh, in_specs=placed, out_specs=P(("seq", "head"), None), check_vma=False
    )
```

time: 151 us -> 127 us (0.84)
  Pallas kernels: 147 us -> 120 us
  local copies, waits for them, and re-layouts: 1.83 us -> 4.9 us
  other arithmetic: 2.36 us -> 0.71 us
    pallas_call x3 -> x1, Pallas kernels: 147 us -> 120 us  [body(): pl.pallas_call(kernel, out_shape=jax.ShapeDtypeStruct((BAND_CORE, 2 * COL...]
    unnamed x7 -> x9, local copies, waits for them, and re-layouts: 1.83 us -> 4.89 us
where the time goes in v3:
time: 127 us; the launch traced here: 126 us
  Pallas kernels  120 us (94%)
  local copies, waits for them, and re-layouts  4.9 us (4%)
    pallas_call x1, Pallas kernels, body(): pl.pallas_call(kernel, out_shape=jax.ShapeDtypeStruct((BAND_CORE, 2 * COL...  120 us
    unnamed x9, local copies, waits for them, and re-layouts  4.89 us

profile of v3, /device:TPU:1, one launch (start us, length us, event | category | flops | bytes accessed | tf_op | source)
XLA Modules:
  0.0 125.8 jit_solution(14204657817322863957)
XLA Ops:
  0.0 0.7 fusion.3
  0.7 0.0 copy-start
  0.7 1.0 copy-done
  1.8 0.0 copy-start.1
  1.8 1.0 copy-done.1
  2.8 0.0 copy-start.2
  2.8 1.0 copy-done.2
  3.8 0.0 copy-start.3
  3.8 1.0 copy-done.3
  4.8 120.1 %sparse_attention.1 = bf16[48,5120]{1,0:T(8,128)(2,1)S(1)} custom-call(s32[8,128]{1,0:T(8,128)S(1)} %pad.4.sel_ref, bf16[3,2,64,640]{3,2,1,0:T(8,128)(2,1)S(1)} %bitcast.3, bf16[6,64,640]{2,1,0:T(8,128)(2,1)S(1)} %bitcast.4, bf16[6,64,640]{2,1,0:T(8,128)(2,1)S(1)} %bitcast.5, bf16[384,640]{1,0:T(8,128)(2,1)S(1)} %copy-done.3, bf16[640,5120]{1,0:T(8,128)(2,1)} %w_ref.1), custom_call_target="tpu_custom_call" | custom-call | tf_op jit(solution)/shard_map/sparse_attention/pallas_call | solution.py:477
  125.0 0.8 copy.8
  (1 shorter events, 0.0 us)
Async XLA Ops:
  0.7 1.0 copy-start
  1.8 1.0 copy-start.1
  2.8 1.0 copy-start.2
  3.8 1.0 copy-start.3

commit v4 on v3

--- a/solution.py
+++ b/solution.py
@@ -29,6 +29,7 @@
 GROUP = 4
 WIDTH = GROUP * CUBE
 LAG = 2
+ROUNDS = ((0,), (1, 7), (2, 6), (3, 5), (4,))
 CONTRACT_LAST = (((1,), (1,)), ((), ()))
 EXP_SCALE = HEAD_DIM ** (-0.5) * math.log2(math.e)
 
@@ -83,11 +84,11 @@
 
 def kernel(
     sel_ref, q_ref, k_ref, v_ref, gate_ref, w_ref, out_ref,
-    kv_ref, qr_ref, qf_ref, all_sel_ref, sel, pooled, scores, o_ref,
+    kv_ref, qr_ref, qf_ref, all_sel_ref, sel, pooled, scores, coarse_scores, o_ref,
     relay_ref, a_ref, att, weight, part, passed, landed, done,
     z_send, z_recv, x_send, x_recv, xq_send, xq_recv, c_send, c_recv,
     sz_send, sz_recv, sx_send, sx_recv, pick_sem,
-    o_send, o_recv, r_send, r_recv, w_sem, t_sem,
+    o_send, o_recv, r_send, r_recv, w_sem, t_send, t_recv,
     part_send, passed_recv, landed_recv, done_send, done_recv,
 ):
     f32, bf16 = jnp.float32, jnp.bfloat16
@@ -127,8 +128,8 @@
         if dz:
             sel_z(n, dz).start()
 
-    def z_copies(act):
-        for n, dz in enumerate(ORDER):
+    def z_copies(act, kinds, dzs):
+        for dz in dzs:
             zt = (z + dz) % NZ
             for cc in range(2):
                 source = k_ref if cc == 0 else v_ref
@@ -136,7 +137,7 @@
                 def one(cond, kind, src, dst):
                     def away():
                         copy = remote(
-                            src, dst, z_send.at[n, cc, kind], z_recv.at[z, kind], zt * NX + x, 2 * y + cc
+                            src, dst, z_send.at[dz, cc, kind], z_recv.at[z, kind], zt * NX + x, 2 * y + cc
                         )
                         if act == "start":
                             copy.start()
@@ -154,38 +155,37 @@
 
                 is_main = c == zt // 5
                 col = pl.ds(pl.multiple_of(zt % 5 * HEAD_DIM, HEAD_DIM), HEAD_DIM)
-                one(is_main, 0, source.at[:, :, col], tile_at(cc, main_slot, z))
                 is_extra = (c == 1) & (zt % 4 != 3)
                 xcol = pl.ds(pl.multiple_of((3 + zt // 4) * HEAD_DIM, HEAD_DIM), HEAD_DIM)
-                one(is_extra, 1, source.at[:, :, xcol], tile_at(cc, extra_slot, z))
-                one(is_main, 2, q_ref.at[:, cc, :, col], qr_ref.at[pl.ds(0, 3), z])
                 rank = zt % 4 - zt % 4 // 3
-                one(is_extra, 3, q_ref.at[rank, cc, :, xcol], qr_ref.at[3, z])
-
-    z_copies("start")
+                if 0 in kinds:
+                    one(is_main, 0, source.at[:, :, col], tile_at(cc, main_slot, z))
+                    one(is_extra, 1, source.at[:, :, xcol], tile_at(cc, extra_slot, z))
+                if 2 in kinds:
+                    one(is_main, 2, q_ref.at[:, cc, :, col], qr_ref.at[pl.ds(0, 3), z])
+                    one(is_extra, 3, q_ref.at[rank, cc, :, xcol], qr_ref.at[3, z])
+
+    tiles, queries = (0, 1), (2, 3)
+    for r in range(2):
+        z_copies("start", tiles, ROUNDS[r])
     w_own.start()
-    w_away.start()
-    for zs in range(NZ):
-        arrived(all_sel_ref.at[x, zs], sz_recv.at[zs])
-    for dx in range(1, NX):
-        sel_x(dx).start()
-
-    def x_copies(n, zs, act):
+    def x_copies(dz, act, kind):
+        zs = (z + dz) % NZ
         for dx in XORDER:
             xt = (x + dx) % NX
-            slot = main_slot + xt // 3 * (4 - main_slot)
+            slot = main_slot if kind == 0 else 4
 
             def away():
                 copy = remote(
                     tile_at(c, slot, zs), tile_at(c, x, zs),
-                    x_send.at[dx, n], x_recv.at[x, zs], z * NX + xt, 2 * y + c,
+                    x_send.at[dx, dz], x_recv.at[x, zs], z * NX + xt, 2 * y + c,
                 )
                 if act == "start":
                     copy.start()
                 else:
                     copy.wait_send()
 
-            pl.when((xt != 3) | has_extra)(away)
+            pl.when(xt != 3 if kind == 0 else (xt == 3) & has_extra)(away)
 
     def core_copy(xs, zs):
         return remote(
@@ -202,40 +202,64 @@
                 arrived(tile_at(c, xs, zs), x_recv.at[xs, zs])
                 core_copy(xs, zs).start()
 
-    for n, dz in enumerate(ORDER):
+    for r, dzs in enumerate(ROUNDS):
+        for dz in dzs:
+            zs = (z + dz) % NZ
+            arrived(tile_at(c, main_slot, zs), z_recv.at[zs, 0])
+            x_copies(dz, "start", 0)
+            pl.when(x != 3)(lambda: core_copy(x, zs).start())
+        if r == 1:
+            z_copies("start", tiles, ROUNDS[2])
+        if r == 3:
+            z_copies("start", tiles, ROUNDS[4])
+        if r == 2:
+            z_copies("start", tiles, ROUNDS[3])
+            for n in range(3):
+                z_copies("start", queries, ROUNDS[n])
+        if r == 3:
+            for n in range(3, 5):
+                z_copies("start", queries, ROUNDS[n])
+        for dz in dzs:
+            zs = (z + dz) % NZ
+            pl.when(has_extra)(lambda: arrived(tile_at(c, extra_slot, zs), z_recv.at[zs, 1]))
+            x_copies(dz, "start", 1)
+            pl.when((x == 3) & has_extra)(lambda: core_copy(x, zs).start())
+        if r == 2:
+            for zs in range(NZ):
+                arrived(all_sel_ref.at[x, zs], sz_recv.at[zs])
+            for dx in range(1, NX):
+                sel_x(dx).start()
+        if r:
+            for dz in ROUNDS[r - 1]:
+                take_x((z + dz) % NZ)
+
+    def xq_copies(dz, act):
         zs = (z + dz) % NZ
-        arrived(tile_at(c, main_slot, zs), z_recv.at[zs, 0])
-        pl.when(has_extra)(lambda: arrived(tile_at(c, extra_slot, zs), z_recv.at[zs, 1]))
-        x_copies(n, zs, "start")
-        pl.when(member)(lambda: core_copy(x, zs).start())
-        if n >= LAG:
-            take_x((z + ORDER[n - LAG]) % NZ)
-
-    for zs in range(NZ):
-        arrived(qr_ref.at[pl.ds(0, 3), zs], z_recv.at[zs, 2])
-        pl.when(has_extra)(lambda: arrived(qr_ref.at[3, zs], z_recv.at[zs, 3]))
-
-    def xq_copies(act):
         for dx in range(NX):
             xt = (x + dx) % NX
 
             def away():
+                src, dst = qr_ref.at[xt, zs], qf_ref.at[x, zs]
                 if dx:
-                    copy = remote(
-                        qr_ref.at[xt], qf_ref.at[x], xq_send.at[dx], xq_recv.at[x], z * NX + xt, 2 * y + c
-                    )
+                    copy = remote(src, dst, xq_send.at[dx, dz], xq_recv.at[x, zs], z * NX + xt, 2 * y + c)
                     if act == "start":
                         copy.start()
                     else:
                         copy.wait_send()
                 elif act == "start":
-                    pltpu.make_async_copy(qr_ref.at[x], qf_ref.at[x], xq_recv.at[x]).start()
+                    pltpu.make_async_copy(src, dst, xq_recv.at[x, zs]).start()
 
             pl.when((xt != 3) | has_extra)(away)
 
-    xq_copies("start")
-    for n in range(NZ - LAG, NZ):
-        take_x((z + ORDER[n]) % NZ)
+    for r, dzs in enumerate(ROUNDS):
+        for dz in dzs:
+            zs = (z + dz) % NZ
+            arrived(qr_ref.at[pl.ds(0, 3), zs], z_recv.at[zs, 2])
+            pl.when(has_extra)(lambda: arrived(qr_ref.at[3, zs], z_recv.at[zs, 3]))
+            xq_copies(dz, "start")
+    for dz in ROUNDS[-1]:
+        take_x((z + dz) % NZ)
+    w_away.start()
 
     for dx in range(1, NX):
         arrived(all_sel_ref.at[(x + dx) % NX], sx_recv.at[(x + dx) % NX])
@@ -245,7 +269,8 @@
     @pl.when(member)
     def _():
         for xs in range(NX):
-            arrived(qf_ref.at[xs], xq_recv.at[xs])
+            for zs in range(NZ):
+                arrived(qf_ref.at[xs, zs], xq_recv.at[xs, zs])
         for xs in range(NX):
             for zs in range(NZ):
                 arrived(tile_at(1 - c, xs, zs), c_recv.at[xs, zs])
@@ -282,15 +307,17 @@
         total = jnp.zeros((2 * CUBE, 128), f32)
         peak = None
         if top is not None:
-            q = jnp.concatenate([qf_ref[2 * pair, zs], qf_ref[2 * pair + 1, zs]], axis=0)
-            s = lax.dot_general(q, pooled[0], CONTRACT_LAST, preferred_element_type=f32)
-            e = jnp.exp2((s - jnp.max(s, axis=1, keepdims=True)) * EXP_SCALE)
+            e = jnp.exp2((coarse_scores[pair] - top[1]) * EXP_SCALE)
             coarse = jnp.dot(e.astype(bf16), pooled[1], preferred_element_type=f32)
             coarse = coarse / jnp.sum(e, axis=1, keepdims=True)
+        q = [qf_ref[2 * pair_ahead + n, zs_ahead] for n in range(2)]
+        s = lax.dot_general(jnp.concatenate(q, axis=0), pooled[0], CONTRACT_LAST, preferred_element_type=f32)
+        coarse_scores[pair_ahead] = s
+        coarse_peak = jnp.max(s, axis=1, keepdims=True)
         zero = jnp.zeros((CUBE, HEAD_DIM), bf16)
         ahead = jnp.concatenate([
-            jnp.concatenate([qf_ref[2 * pair_ahead, zs_ahead], zero], axis=1),
-            jnp.concatenate([zero, qf_ref[2 * pair_ahead + 1, zs_ahead]], axis=1),
+            jnp.concatenate([q[0], zero], axis=1),
+            jnp.concatenate([zero, q[1]], axis=1),
         ], axis=0)
         for g in range(TOPK // GROUP):
             cols = slice(g * WIDTH, (g + 1) * WIDTH)
@@ -299,15 +326,15 @@
             part_peak = jnp.maximum(s[:, :128], s[:, 128:])
             peak = part_peak if peak is None else jnp.maximum(peak, part_peak)
             if top is not None:
-                e = jnp.exp2((scores[pair, :, cols] - top) * EXP_SCALE)
+                e = jnp.exp2((scores[pair, :, cols] - top[0]) * EXP_SCALE)
                 total = total + (e[:, :128] + e[:, 128:])
                 out = jnp.dot(e.astype(bf16), pair_rows(1, pair, zs, g), preferred_element_type=f32)
                 acc = [acc[0] + out[:CUBE, :HEAD_DIM], acc[1] + out[CUBE:, HEAD_DIM:]]
         if top is not None:
             mixed = jnp.concatenate(acc, axis=0) / jnp.sum(total, axis=1, keepdims=True) + coarse
             for n in range(2):
-                o_ref[2 * pair + n, zs] = mixed[n * CUBE:(n + 1) * CUBE].astype(bf16)
-        return jnp.max(peak, axis=1, keepdims=True)
+                o_ref[2 * pair + n, zs] = mixed[n * CUBE:(n + 1) * CUBE].astype(bf16).reshape(2, CUBE // 2, HEAD_DIM)
+        return jnp.max(peak, axis=1, keepdims=True), coarse_peak
 
     def o_copy(dx, n, zs):
         xt = (x + dx) % NX
@@ -332,10 +359,10 @@
                 )
 
         col = pl.ds(pl.multiple_of(z % 5 * HEAD_DIM, HEAD_DIM), HEAD_DIM)
-        one(z >= 0, 0, z // 5, relay_ref.at[pl.ds(0, 3), zs], a_ref.at[:, c, :, col])
+        one(z >= 0, 0, z // 5, relay_ref.at[pl.ds(0, 3), zs], a_ref.at[:, c, :, :, col])
         xcol = pl.ds(pl.multiple_of((3 + z // 4) * HEAD_DIM, HEAD_DIM), HEAD_DIM)
         third = z % 4 - z % 4 // 3
-        one(has_extra, 1, 1, relay_ref.at[3, zs], a_ref.at[third, c, :, xcol])
+        one(has_extra, 1, 1, relay_ref.at[3, zs], a_ref.at[third, c, :, :, xcol])
 
     def pass_on(n):
         zs = target(n)
@@ -365,21 +392,36 @@
     for zs in range(NZ):
         for cc in range(2):
             col = pl.ds(zs % 5 * HEAD_DIM, HEAD_DIM)
-            pl.when(c == zs // 5)(lambda: arrived(a_ref.at[:, cc, :, col], r_recv.at[zs, cc, 0]))
+            pl.when(c == zs // 5)(lambda: arrived(a_ref.at[:, cc, :, :, col], r_recv.at[zs, cc, 0]))
             if zs % 4 != 3:
                 xcol = pl.ds((3 + zs // 4) * HEAD_DIM, HEAD_DIM)
-                pl.when(c == 1)(lambda: arrived(a_ref.at[zs % 4, cc, :, xcol], r_recv.at[zs, cc, 1]))
-
-    mixed = a_ref[...].reshape(ROWS, FEATS).astype(f32)
-    att[c] = (jax.nn.sigmoid(gate_ref[...].astype(f32)) * mixed).astype(bf16)
-    att_away = remote(att.at[c], att.at[c], t_sem.at[0], t_sem.at[1], here, sibling)
-    att_away.start()
+                pl.when(c == 1)(lambda: arrived(a_ref.at[zs % 4, cc, :, :, xcol], r_recv.at[zs, cc, 1]))
+
+    def band_rows(band):
+        return pl.ds(pl.multiple_of(band * BAND, BAND), BAND)
+
+    def att_away(n, band):
+        return remote(
+            att.at[c, band_rows(band)], att.at[c, band_rows(band)], t_send.at[n], t_recv.at[n], here, sibling
+        )
+
+    bands = [(y + dy) % NY for dy in (2, 1, 3, 0)]
+    for n, band in enumerate(bands):
+        for piece in range(3):
+            part_of = band * 3 + piece
+            mixed = a_ref[part_of // 4, part_of // 2 % 2, part_of % 2].astype(f32)
+            gates = jax.nn.sigmoid(gate_ref[part_of].astype(f32))
+            start = pl.multiple_of(part_of * (CUBE // 2), CUBE // 2)
+            att[c, pl.ds(start, CUBE // 2), :] = (gates * mixed).astype(bf16)
+        att_away(n, band).start()
     w_own.wait()
     arrived(weight.at[block(1 - c)], w_sem.at[2])
-    arrived(att.at[1 - c], t_sem.at[1])
+
+    def band_here(n):
+        arrived(att.at[1 - c, band_rows(bands[n])], t_recv.at[n])
 
     def product(band, t):
-        rows = pl.ds(pl.multiple_of(band * BAND, BAND), BAND)
+        rows = band_rows(band)
         cols = slice(t * TILE, (t + 1) * TILE)
         total = jnp.dot(att[0, rows, :], weight[:FEATS, cols], preferred_element_type=f32)
         return total + jnp.dot(att[1, rows, :], weight[FEATS:, cols], preferred_element_type=f32)
@@ -398,9 +440,12 @@
             here, 2 * (left if side else right) + c,
         )
 
+    band_here(0)
     for t in (0, 2, 1, 3):
         part[1, t] = product((y + 2) % NY, t).astype(bf16)
         across(t).start()
+    band_here(1)
+    band_here(2)
     for side, t in ((0, 2), (1, 0), (0, 3), (1, 1)):
         part[2 * side, t] = product(left if side else right, t).astype(bf16)
         onward(side, t).start()
@@ -425,6 +470,7 @@
     def keep(t):
         return pltpu.make_async_copy(done.at[t, rows_of(c)], out_ref.at[:, columns(c, t)], done_send.at[1, t])
 
+    band_here(3)
     for t in (2, 0, 3, 1):
         total = product(y, t)
         for side in range(2):
@@ -442,7 +488,8 @@
         for side in range(2):
             onward(side, t).wait_send()
     w_away.wait_send()
-    att_away.wait_send()
+    for n, band in enumerate(bands):
+        att_away(n, band).wait_send()
 
     @pl.when(member)
     def _():
@@ -460,10 +507,11 @@
     for n, dz in enumerate(ORDER):
         if dz:
             sel_z(n, dz).wait_send()
-    z_copies("wait")
-    for n, dz in enumerate(ORDER):
-        x_copies(n, (z + dz) % NZ, "wait")
-    xq_copies("wait")
+    for dz in range(NZ):
+        z_copies("wait", tiles + queries, (dz,))
+        x_copies(dz, "wait", 0)
+        x_copies(dz, "wait", 1)
+        xq_copies(dz, "wait")
 
 
 def body(query_states, key_states, value_states, gate_states, selection, out_weight):
@@ -474,6 +522,7 @@
     places = (owner % NX * NZ + owner // NX) * CUBE_DEV + selection % CUBE_DEV
     places = jnp.pad(places, ((0, 8 - CUBE_DEV), (0, 128 - TOPK)))
     cubes = vmem((NX, NZ, CUBE, HEAD_DIM), bf16)
+    halves = vmem((NX, NZ, 2, CUBE // 2, HEAD_DIM), bf16)
     return pl.pallas_call(
         kernel,
         out_shape=jax.ShapeDtypeStruct((BAND_CORE, 2 * COLS), bf16),
@@ -487,9 +536,10 @@
             pltpu.SMEM((NX, NZ, 8, 128), jnp.int32),
             vmem((2, N_CUBES, HEAD_DIM), bf16),
             vmem((2, 2 * CUBE, TOPK * CUBE), jnp.float32),
-            cubes,
-            cubes,
-            vmem((3, 2, CUBE, FEATS), bf16),
+            vmem((2, 2 * CUBE, N_CUBES), jnp.float32),
+            halves,
+            halves,
+            vmem((3, 2, 2, CUBE // 2, FEATS), bf16),
             vmem((2, ROWS, FEATS), bf16),
             vmem((2 * FEATS, COLS), bf16),
             vmem((3, TILES, BAND, TILE), bf16),
@@ -498,14 +548,14 @@
             vmem((TILES, BAND, TILE), bf16),
             dma((NZ, 2, 4)), dma((NZ, 4)),
             dma((NX, NZ)), dma((NX, NZ)),
-            dma((NX,)), dma((NX,)),
+            dma((NX, NZ)), dma((NX, NZ)),
             dma((NX, NZ)), dma((NX, NZ)),
             dma((NZ,)), dma((NZ,)), dma((NX,)), dma((NX,)), dma,
-            dma((NX, NZ)), dma((NX, NZ)), dma((NZ, 2)), dma((NZ, 2, 2)), dma((3,)), dma((2,)),
+            dma((NX, NZ)), dma((NX, NZ)), dma((NZ, 2)), dma((NZ, 2, 2)), dma((3,)), dma((NY,)), dma((NY,)),
             dma((3, TILES)), dma((TILES,)), dma((2, TILES)), dma((2, TILES)), dma((TILES,)),
         ],
         compiler_params=pltpu.CompilerParams(
-            collective_id=0, has_side_effects=True, vmem_limit_bytes=48 * 2**20
+            collective_id=0, has_side_effects=True, vmem_limit_bytes=60 * 2**20
         ),
         name="sparse_attention",
     )(
@@ -513,7 +563,7 @@
         query_states.reshape(3, 2, CUBE, FEATS),
         key_states.reshape(CUBE_DEV, CUBE, FEATS),
         value_states.reshape(CUBE_DEV, CUBE, FEATS),
-        gate_states,
+        gate_states.reshape(2 * CUBE_DEV, CUBE // 2, FEATS),
         out_weight,
     )
 

time: 127 us -> 115 us (0.906)
  Pallas kernels: 120 us -> 112 us
  local copies, waits for them, and re-layouts: 4.9 us -> 2.44 us
    pallas_call x1, Pallas kernels: 120 us -> 112 us  [body(): pl.pallas_call(kernel, out_shape=jax.ShapeDtypeStruct((BAND_CORE, 2 * COL...]
    unnamed x9 -> x1, local copies, waits for them, and re-layouts: 4.89 us -> 1.84 us
where the time goes in v4:
time: 115 us
  Pallas kernels  112 us (97%)
  local copies, waits for them, and re-layouts  2.44 us (2%)
    pallas_call x1, Pallas kernels, body(): pl.pallas_call(kernel, out_shape=jax.ShapeDtypeStruct((BAND_CORE, 2 * COL...  112 us

profile of v4, /device:TPU:1, one launch (start us, length us, event | category | flops | bytes accessed | tf_op | source)
XLA Modules:
  0.0 114.9 jit_solution(6433491267084292666)
XLA Ops:
  0.0 0.7 fusion.3
  0.7 0.6 pad.4.sel_ref
  1.3 111.7 %sparse_attention.1 = bf16[48,5120]{1,0:T(8,128)(2,1)} custom-call(s32[8,128]{1,0:T(8,128)} %pad.4.sel_ref, bf16[3,2,64,640]{3,2,1,0:T(8,128)(2,1)} %bitcast.4, bf16[6,64,640]{2,1,0:T(8,128)(2,1)} %bitcast.5, bf16[6,64,640]{2,1,0:T(8,128)(2,1)} %bitcast.6, bf16[12,32,640]{2,1,0:T(8,128)(2,1)} %bitcast.7, bf16[640,5120]{1,0:T(8,128)(2,1)} %w_ref.1), custom_call_target="tpu_custom_call" | custom-call | tf_op jit(solution)/shard_map/sparse_attention/pallas_call | solution.py:526
  113.0 1.8 %copy.8 = bf16[48,5120]{1,0:T(8,128)(2,1)} copy(bf16[48,5120]{1,0:T(8,128)(2,1)} %sparse_attention.1) | data formatting | bytes 983040

commit v5 on v4

--- a/solution.py
+++ b/solution.py
@@ -83,12 +83,12 @@
 
 
 def kernel(
-    sel_ref, q_ref, k_ref, v_ref, gate_ref, w_ref, out_ref,
+    sel_ref, q_ref, k_ref, v_ref, gate_hbm, w_ref, out_ref,
     kv_ref, qr_ref, qf_ref, all_sel_ref, sel, pooled, scores, coarse_scores, o_ref,
-    relay_ref, a_ref, att, weight, part, passed, landed, done,
+    relay_ref, a_ref, gate_ref, att, weight, part, passed, landed, done,
     z_send, z_recv, x_send, x_recv, xq_send, xq_recv, c_send, c_recv,
     sz_send, sz_recv, sx_send, sx_recv, pick_sem,
-    o_send, o_recv, r_send, r_recv, w_sem, t_send, t_recv,
+    o_send, o_recv, r_send, r_recv, gate_sem, w_sem, t_send, t_recv,
     part_send, passed_recv, landed_recv, done_send, done_recv,
 ):
     f32, bf16 = jnp.float32, jnp.bfloat16
@@ -115,15 +115,15 @@
 
     def sel_z(n, dz):
         return remote(
-            sel_ref, all_sel_ref.at[x, z], sz_send.at[n], sz_recv.at[z], (z + dz) % NZ * NX + x, 2 * y + c
+            sel_ref, all_sel_ref.at[x, z], sz_send, sz_recv, (z + dz) % NZ * NX + x, 2 * y + c
         )
 
     def sel_x(dx):
         return remote(
-            all_sel_ref.at[x], all_sel_ref.at[x], sx_send.at[dx], sx_recv.at[x], z * NX + (x + dx) % NX, 2 * y + c
-        )
-
-    pltpu.make_async_copy(sel_ref, all_sel_ref.at[x, z], sz_recv.at[z]).start()
+            all_sel_ref.at[x], all_sel_ref.at[x], sx_send, sx_recv, z * NX + (x + dx) % NX, 2 * y + c
+        )
+
+    pltpu.make_async_copy(sel_ref, all_sel_ref.at[x, z], sz_recv).start()
     for n, dz in enumerate(ORDER):
         if dz:
             sel_z(n, dz).start()
@@ -169,6 +169,8 @@
     for r in range(2):
         z_copies("start", tiles, ROUNDS[r])
     w_own.start()
+    gate_in = pltpu.make_async_copy(gate_hbm, gate_ref, gate_sem)
+    gate_in.start()
     def x_copies(dz, act, kind):
         zs = (z + dz) % NZ
         for dx in XORDER:
@@ -178,7 +180,7 @@
             def away():
                 copy = remote(
                     tile_at(c, slot, zs), tile_at(c, x, zs),
-                    x_send.at[dx, dz], x_recv.at[x, zs], z * NX + xt, 2 * y + c,
+                    x_send, x_recv.at[zs], z * NX + xt, 2 * y + c,
                 )
                 if act == "start":
                     copy.start()
@@ -190,16 +192,16 @@
     def core_copy(xs, zs):
         return remote(
             tile_at(c, xs, zs), tile_at(c, xs, zs),
-            c_send.at[xs, zs], c_recv.at[xs, zs], here, sibling,
+            c_send, c_recv, here, sibling,
         )
 
     def take_x(zs):
+        pl.when(member)(lambda: arrived(kv_ref.at[c, pl.ds(0, 3 * CUBE_DEV)], x_recv.at[zs]))
         for dx in XORDER:
             xs = (x + dx) % NX
 
             @pl.when(member)
             def _():
-                arrived(tile_at(c, xs, zs), x_recv.at[xs, zs])
                 core_copy(xs, zs).start()
 
     for r, dzs in enumerate(ROUNDS):
@@ -225,8 +227,7 @@
             x_copies(dz, "start", 1)
             pl.when((x == 3) & has_extra)(lambda: core_copy(x, zs).start())
         if r == 2:
-            for zs in range(NZ):
-                arrived(all_sel_ref.at[x, zs], sz_recv.at[zs])
+            arrived(all_sel_ref.at[x], sz_recv)
             for dx in range(1, NX):
                 sel_x(dx).start()
         if r:
@@ -241,15 +242,19 @@
             def away():
                 src, dst = qr_ref.at[xt, zs], qf_ref.at[x, zs]
                 if dx:
-                    copy = remote(src, dst, xq_send.at[dx, dz], xq_recv.at[x, zs], z * NX + xt, 2 * y + c)
+                    copy = remote(src, dst, xq_send, xq_recv, z * NX + xt, 2 * y + c)
                     if act == "start":
                         copy.start()
                     else:
                         copy.wait_send()
                 elif act == "start":
-                    pltpu.make_async_copy(src, dst, xq_recv.at[x, zs]).start()
+                    pltpu.make_async_copy(src, dst, xq_recv).start()
 
             pl.when((xt != 3) | has_extra)(away)
+
+    arrived(all_sel_ref.at[pl.ds(0, NX - 1)], sx_recv)
+    picks = pltpu.make_async_copy(all_sel_ref, sel, pick_sem)
+    picks.start()
 
     for r, dzs in enumerate(ROUNDS):
         for dz in dzs:
@@ -261,19 +266,10 @@
         take_x((z + dz) % NZ)
     w_away.start()
 
-    for dx in range(1, NX):
-        arrived(all_sel_ref.at[(x + dx) % NX], sx_recv.at[(x + dx) % NX])
-    picks = pltpu.make_async_copy(all_sel_ref, sel, pick_sem)
-    picks.start()
-
     @pl.when(member)
     def _():
-        for xs in range(NX):
-            for zs in range(NZ):
-                arrived(qf_ref.at[xs, zs], xq_recv.at[xs, zs])
-        for xs in range(NX):
-            for zs in range(NZ):
-                arrived(tile_at(1 - c, xs, zs), c_recv.at[xs, zs])
+        arrived(qf_ref, xq_recv)
+        arrived(kv_ref.at[1 - c, pl.ds(0, N_CUBES)], c_recv)
 
     picks.wait()
 
@@ -339,13 +335,13 @@
     def o_copy(dx, n, zs):
         xt = (x + dx) % NX
         return remote(
-            o_ref.at[xt, zs], relay_ref.at[x, zs], o_send.at[dx, n], o_recv.at[x, zs], z * NX + xt, 2 * y + c
+            o_ref.at[xt, zs], relay_ref.at[x, zs], o_send, o_recv.at[zs], z * NX + xt, 2 * y + c
         )
 
     def pass_copies(n, zs, act):
         def one(cond, kind, core, src, dst):
             def away():
-                copy = remote(src, dst, r_send.at[n, kind], r_recv.at[z, c, kind], zs * NX + x, 2 * y + core)
+                copy = remote(src, dst, r_send.at[n, kind], r_recv, zs * NX + x, 2 * y + core)
                 if act == "start":
                     copy.start()
                 else:
@@ -355,7 +351,7 @@
             pl.when(cond & jnp.logical_not(stays))(away)
             if act == "start":
                 pl.when(cond & stays)(
-                    lambda: pltpu.make_async_copy(src, dst, r_recv.at[z, c, kind]).start()
+                    lambda: pltpu.make_async_copy(src, dst, r_recv).start()
                 )
 
         col = pl.ds(pl.multiple_of(z % 5 * HEAD_DIM, HEAD_DIM), HEAD_DIM)
@@ -366,9 +362,8 @@
 
     def pass_on(n):
         zs = target(n)
-        for xs in range(3):
-            arrived(relay_ref.at[xs, zs], o_recv.at[xs, zs])
-        pl.when(has_extra)(lambda: arrived(relay_ref.at[3, zs], o_recv.at[3, zs]))
+        pl.when(has_extra)(lambda: arrived(relay_ref.at[:, zs], o_recv.at[zs]))
+        pl.when(jnp.logical_not(has_extra))(lambda: arrived(relay_ref.at[pl.ds(0, 3), zs], o_recv.at[zs]))
         pass_copies(n, zs, "start")
 
     def step(n, top):
@@ -378,7 +373,7 @@
 
         @pl.when(member)
         def _():
-            pltpu.make_async_copy(o_ref.at[x, zs], relay_ref.at[x, zs], o_recv.at[x, zs]).start()
+            pltpu.make_async_copy(o_ref.at[x, zs], relay_ref.at[x, zs], o_recv.at[zs]).start()
             for dx in XORDER:
                 o_copy(dx, n, zs).start()
 
@@ -389,20 +384,15 @@
     for n in range(NZ - LAG, NZ):
         pass_on(n)
 
-    for zs in range(NZ):
-        for cc in range(2):
-            col = pl.ds(zs % 5 * HEAD_DIM, HEAD_DIM)
-            pl.when(c == zs // 5)(lambda: arrived(a_ref.at[:, cc, :, :, col], r_recv.at[zs, cc, 0]))
-            if zs % 4 != 3:
-                xcol = pl.ds((3 + zs // 4) * HEAD_DIM, HEAD_DIM)
-                pl.when(c == 1)(lambda: arrived(a_ref.at[zs % 4, cc, :, :, xcol], r_recv.at[zs, cc, 1]))
+    gate_in.wait()
+    arrived(a_ref, r_recv)
 
     def band_rows(band):
         return pl.ds(pl.multiple_of(band * BAND, BAND), BAND)
 
     def att_away(n, band):
         return remote(
-            att.at[c, band_rows(band)], att.at[c, band_rows(band)], t_send.at[n], t_recv.at[n], here, sibling
+            att.at[c, band_rows(band)], att.at[c, band_rows(band)], t_send, t_recv.at[n], here, sibling
         )
 
     bands = [(y + dy) % NY for dy in (2, 1, 3, 0)]
@@ -430,13 +420,13 @@
 
     def across(t):
         return remote(
-            part.at[1, t], passed.at[t], part_send.at[1, t], passed_recv.at[t],
+            part.at[1, t], passed.at[t], part_send.at[0], passed_recv.at[t],
             here, 2 * (right if t < 2 else left) + c,
         )
 
     def onward(side, t):
         return remote(
-            part.at[2 * side, t], landed.at[side, t], part_send.at[2 * side, t], landed_recv.at[side, t],
+            part.at[2 * side, t], landed.at[side, t], part_send.at[1], landed_recv.at[side, t],
             here, 2 * (left if side else right) + c,
         )
 
@@ -449,6 +439,30 @@
     for side, t in ((0, 2), (1, 0), (0, 3), (1, 1)):
         part[2 * side, t] = product(left if side else right, t).astype(bf16)
         onward(side, t).start()
+    @pl.when(member)
+    def _():
+        arrived(o_ref.at[pl.ds(0, 3)], o_send)
+        arrived(kv_ref.at[c, pl.ds(0, N_CUBES)], c_send)
+
+    for n in range(NZ):
+        pass_copies(n, target(n), "wait")
+    arrived(all_sel_ref.at[pl.ds(0, NX - 1)], sx_send)
+    arrived(all_sel_ref.at[x, pl.ds(0, NZ - 1)], sz_send)
+    for dz in range(NZ):
+        z_copies("wait", tiles + queries, (dz,))
+
+    to_three = (x == 3) | has_extra
+
+    @pl.when(to_three)
+    def _():
+        arrived(kv_ref.at[c, pl.ds(0, 3 * NZ * CUBE_DEV)], x_send)
+        arrived(qf_ref.at[pl.ds(0, 3)], xq_send)
+
+    @pl.when(jnp.logical_not(to_three))
+    def _():
+        arrived(kv_ref.at[c, pl.ds(0, 2 * NZ * CUBE_DEV)], x_send)
+        arrived(qf_ref.at[pl.ds(0, 2)], xq_send)
+
     for side, t in ((0, 0), (1, 2), (0, 1), (1, 3)):
         total = product(left if side else right, t)
         arrived(passed.at[t], passed_recv.at[t])
@@ -464,11 +478,11 @@
     def give(t):
         return remote(
             done.at[t, rows_of(1 - c)], out_ref.at[:, columns(c, t)],
-            done_send.at[0, t], done_recv.at[t], here, 2 * y + 1 - c,
+            done_send.at[0], done_recv, here, 2 * y + 1 - c,
         )
 
     def keep(t):
-        return pltpu.make_async_copy(done.at[t, rows_of(c)], out_ref.at[:, columns(c, t)], done_send.at[1, t])
+        return pltpu.make_async_copy(done.at[t, rows_of(c)], out_ref.at[:, columns(c, t)], done_send.at[1])
 
     band_here(3)
     for t in (2, 0, 3, 1):
@@ -480,38 +494,13 @@
         give(t).start()
         keep(t).start()
 
-    for t in range(TILES):
-        give(t).wait_send()
-        keep(t).wait()
-        arrived(out_ref.at[:, columns(1 - c, t)], done_recv.at[t])
-        across(t).wait_send()
-        for side in range(2):
-            onward(side, t).wait_send()
+    arrived(passed, part_send.at[0])
+    arrived(landed, part_send.at[1])
+    arrived(out_ref.at[:, half(c)], done_send.at[0])
+    arrived(out_ref.at[:, half(c)], done_send.at[1])
+    arrived(out_ref.at[:, half(1 - c)], done_recv)
     w_away.wait_send()
-    for n, band in enumerate(bands):
-        att_away(n, band).wait_send()
-
-    @pl.when(member)
-    def _():
-        for n in range(NZ):
-            for dx in XORDER:
-                o_copy(dx, n, target(n)).wait_send()
-        for xs in range(NX):
-            for zs in range(NZ):
-                core_copy(xs, zs).wait_send()
-
-    for n in range(NZ):
-        pass_copies(n, target(n), "wait")
-    for dx in range(1, NX):
-        sel_x(dx).wait_send()
-    for n, dz in enumerate(ORDER):
-        if dz:
-            sel_z(n, dz).wait_send()
-    for dz in range(NZ):
-        z_copies("wait", tiles + queries, (dz,))
-        x_copies(dz, "wait", 0)
-        x_copies(dz, "wait", 1)
-        xq_copies(dz, "wait")
+    arrived(att.at[c], t_send)
 
 
 def body(query_states, key_states, value_states, gate_states, selection, out_weight):
@@ -526,7 +515,7 @@
     return pl.pallas_call(
         kernel,
         out_shape=jax.ShapeDtypeStruct((BAND_CORE, 2 * COLS), bf16),
-        in_specs=[any_spec] * 4 + [pl.BlockSpec(memory_space=pltpu.VMEM), any_spec],
+        in_specs=[any_spec] * 6,
         out_specs=any_spec,
         scratch_shapes=[
             vmem((2, 5 * NZ * CUBE_DEV, CUBE, HEAD_DIM), bf16),
@@ -540,6 +529,7 @@
             halves,
             halves,
             vmem((3, 2, 2, CUBE // 2, FEATS), bf16),
+            vmem((2 * CUBE_DEV, CUBE // 2, FEATS), bf16),
             vmem((2, ROWS, FEATS), bf16),
             vmem((2 * FEATS, COLS), bf16),
             vmem((3, TILES, BAND, TILE), bf16),
@@ -547,12 +537,10 @@
             vmem((2, TILES, BAND, TILE), bf16),
             vmem((TILES, BAND, TILE), bf16),
             dma((NZ, 2, 4)), dma((NZ, 4)),
-            dma((NX, NZ)), dma((NX, NZ)),
-            dma((NX, NZ)), dma((NX, NZ)),
-            dma((NX, NZ)), dma((NX, NZ)),
-            dma((NZ,)), dma((NZ,)), dma((NX,)), dma((NX,)), dma,
-            dma((NX, NZ)), dma((NX, NZ)), dma((NZ, 2)), dma((NZ, 2, 2)), dma((3,)), dma((NY,)), dma((NY,)),
-            dma((3, TILES)), dma((TILES,)), dma((2, TILES)), dma((2, TILES)), dma((TILES,)),
+            dma, dma((NZ,)), dma, dma, dma, dma,
+            dma, dma, dma, dma, dma,
+            dma, dma((NZ,)), dma((NZ, 2)), dma, dma, dma((3,)), dma, dma((NY,)),
+            dma((2,)), dma((TILES,)), dma((2, TILES)), dma((2,)), dma,
         ],
         compiler_params=pltpu.CompilerParams(
             collective_id=0, has_side_effects=True, vmem_limit_bytes=60 * 2**20

time: 115 us -> 111 us (0.965)
  Pallas kernels: 112 us -> 107 us
    pallas_call x1, Pallas kernels: 112 us -> 107 us  [body(): pl.pallas_call(kernel, out_shape=jax.ShapeDtypeStruct((BAND_CORE, 2 * COL...]
where the time goes in v5:
time: 111 us; the launch traced here: 110 us
  Pallas kernels  107 us (96%)
  local copies, waits for them, and re-layouts  2.44 us (2%)
    pallas_call x1, Pallas kernels, body(): pl.pallas_call(kernel, out_shape=jax.ShapeDtypeStruct((BAND_CORE, 2 * COL...  107 us

profile of v5, /device:TPU:1, one launch (start us, length us, event | category | flops | bytes accessed | tf_op | source)
XLA Modules:
  0.0 110.4 jit_solution(17159703301515457892)
XLA Ops:
  0.0 0.7 fusion.3
  0.7 0.6 pad.4.sel_ref
  1.3 107.3 %sparse_attention.1 = bf16[48,5120]{1,0:T(8,128)(2,1)} custom-call(s32[8,128]{1,0:T(8,128)} %pad.4.sel_ref, bf16[3,2,64,640]{3,2,1,0:T(8,128)(2,1)} %bitcast.4, bf16[6,64,640]{2,1,0:T(8,128)(2,1)} %bitcast.5, bf16[6,64,640]{2,1,0:T(8,128)(2,1)} %bitcast.6, bf16[12,32,640]{2,1,0:T(8,128)(2,1)} %bitcast.7, bf16[640,5120]{1,0:T(8,128)(2,1)} %w_ref.1), custom_call_target="tpu_custom_call" | custom-call | tf_op jit(solution)/shard_map/sparse_attention/pallas_call | solution.py:515
  108.6 1.8 %copy.8 = bf16[48,5120]{1,0:T(8,128)(2,1)} copy(bf16[48,5120]{1,0:T(8,128)(2,1)} %sparse_attention.1) | data formatting | bytes 983040

commit v6 on v5

--- a/solution.py
+++ b/solution.py
@@ -28,7 +28,7 @@
 N_CUBES = NZ * NX * CUBE_DEV
 GROUP = 4
 WIDTH = GROUP * CUBE
-LAG = 2
+LAG = 3
 ROUNDS = ((0,), (1, 7), (2, 6), (3, 5), (4,))
 CONTRACT_LAST = (((1,), (1,)), ((), ()))
 EXP_SCALE = HEAD_DIM ** (-0.5) * math.log2(math.e)
@@ -266,24 +266,26 @@
         take_x((z + dz) % NZ)
     w_away.start()
 
+    def pool(which):
+        def some(i, _):
+            sums = jnp.sum(kv_ref[which, pl.ds(i * 16, 16)].astype(f32), axis=1)
+            pooled[which, pl.ds(pl.multiple_of(i * 16, 16), 16), :] = (sums * (1.0 / CUBE)).astype(bf16)
+            return 0
+
+        lax.fori_loop(0, N_CUBES // 16, some, 0)
+
+    pool(c)
+
     @pl.when(member)
     def _():
         arrived(qf_ref, xq_recv)
         arrived(kv_ref.at[1 - c, pl.ds(0, N_CUBES)], c_recv)
 
+    pool(1 - c)
     picks.wait()
 
     rank = x + x // 3 * (z % 4 - x)
     cube = rank * 2 + c - rank // 3 * 2
-
-    def pool(i, _):
-        for which in range(2):
-            block_of = kv_ref[which, pl.ds(i * 16, 16)].astype(f32)
-            sums = jnp.sum(block_of, axis=1)
-            pooled[which, pl.ds(pl.multiple_of(i * 16, 16), 16), :] = (sums * (1.0 / CUBE)).astype(bf16)
-        return 0
-
-    lax.fori_loop(0, N_CUBES // 16, pool, 0)
 
     def target(n):
         return (z + 4 + (1 - n % 2 * 2) * ((n + 1) // 2)) % NZ
@@ -507,9 +509,9 @@
     bf16 = jnp.bfloat16
     any_spec = pl.BlockSpec(memory_space=pl.ANY)
     dma, vmem = pltpu.SemaphoreType.DMA, pltpu.VMEM
-    owner = selection // CUBE_DEV
-    places = (owner % NX * NZ + owner // NX) * CUBE_DEV + selection % CUBE_DEV
-    places = jnp.pad(places, ((0, 8 - CUBE_DEV), (0, 128 - TOPK)))
+    padded = jnp.pad(selection, ((0, 8 - CUBE_DEV), (0, 128 - TOPK)))
+    owner = padded // CUBE_DEV
+    places = (owner % NX * NZ + owner // NX) * CUBE_DEV + padded % CUBE_DEV
     cubes = vmem((NX, NZ, CUBE, HEAD_DIM), bf16)
     halves = vmem((NX, NZ, 2, CUBE // 2, HEAD_DIM), bf16)
     return pl.pallas_call(

time: 111 us -> 110 us (level)
  no operation moved by 1% of the time
where the time goes in v6:
time: 110 us; the launch traced here: 109 us
  Pallas kernels  106 us (96%)
  local copies, waits for them, and re-layouts  1.84 us (2%)
  other arithmetic  1.3 us (1%)
    pallas_call x1, Pallas kernels, body(): pl.pallas_call(kernel, out_shape=jax.ShapeDtypeStruct((BAND_CORE, 2 * COL...  106 us

profile of v6, /device:TPU:1, one launch (start us, length us, event | category | flops | bytes accessed | tf_op | source)
XLA Modules:
  0.0 109.4 jit_solution(1116386188671040207)
XLA Ops:
  0.0 1.3 %fusion.3.sel_ref = s32[8,128]{1,0:T(8,128)} fusion(s32[6,32]{1,0:T(8,128)} %param.10), kind=kLoop, calls=%fused_computation.10 | loop fusion | flops 35840 | bytes 4864 | tf_op jit(solution)/shard_map/add | solution.py:514
  1.3 106.2 %sparse_attention.1 = bf16[48,5120]{1,0:T(8,128)(2,1)} custom-call(s32[8,128]{1,0:T(8,128)} %fusion.3.sel_ref, bf16[3,2,64,640]{3,2,1,0:T(8,128)(2,1)} %bitcast.4, bf16[6,64,640]{2,1,0:T(8,128)(2,1)} %bitcast.5, bf16[6,64,640]{2,1,0:T(8,128)(2,1)} %bitcast.6, bf16[12,32,640]{2,1,0:T(8,128)(2,1)} %bitcast.7, bf16[640,5120]{1,0:T(8,128)(2,1)} %w_ref.1), custom_call_target="tpu_custom_call" | custom-call | tf_op jit(solution)/shard_map/sparse_attention/pallas_call | solution.py:517
  107.5 1.8 %copy.8 = bf16[48,5120]{1,0:T(8,128)(2,1)} copy(bf16[48,5120]{1,0:T(8,128)(2,1)} %sparse_attention.1) | data formatting | bytes 983040

commit v7 on v6

--- a/solution.py
+++ b/solution.py
@@ -28,7 +28,7 @@
 N_CUBES = NZ * NX * CUBE_DEV
 GROUP = 4
 WIDTH = GROUP * CUBE
-LAG = 3
+LAG = 4
 ROUNDS = ((0,), (1, 7), (2, 6), (3, 5), (4,))
 CONTRACT_LAST = (((1,), (1,)), ((), ()))
 EXP_SCALE = HEAD_DIM ** (-0.5) * math.log2(math.e)

time: 110 us -> 111 us (level)
  Pallas kernels: 106 us -> 108 us
    pallas_call x1, Pallas kernels: 106 us -> 108 us  [body(): pl.pallas_call(kernel, out_shape=jax.ShapeDtypeStruct((BAND_CORE, 2 * COL...]
where the time goes in v7:
time: 111 us
  Pallas kernels  108 us (97%)
  local copies, waits for them, and re-layouts  1.84 us (2%)
  other arithmetic  1.3 us (1%)
    pallas_call x1, Pallas kernels, body(): pl.pallas_call(kernel, out_shape=jax.ShapeDtypeStruct((BAND_CORE, 2 * COL...  108 us

profile of v7, /device:TPU:1, one launch (start us, length us, event | category | flops | bytes accessed | tf_op | source)
XLA Modules:
  0.0 110.8 jit_solution(16393495020219503502)
XLA Ops:
  0.0 1.3 %fusion.3.sel_ref = s32[8,128]{1,0:T(8,128)} fusion(s32[6,32]{1,0:T(8,128)} %param.10), kind=kLoop, calls=%fused_computation.10 | loop fusion | flops 35840 | bytes 4864 | tf_op jit(solution)/shard_map/add | solution.py:514
  1.3 107.6 %sparse_attention.1 = bf16[48,5120]{1,0:T(8,128)(2,1)} custom-call(s32[8,128]{1,0:T(8,128)} %fusion.3.sel_ref, bf16[3,2,64,640]{3,2,1,0:T(8,128)(2,1)} %bitcast.4, bf16[6,64,640]{2,1,0:T(8,128)(2,1)} %bitcast.5, bf16[6,64,640]{2,1,0:T(8,128)(2,1)} %bitcast.6, bf16[12,32,640]{2,1,0:T(8,128)(2,1)} %bitcast.7, bf16[640,5120]{1,0:T(8,128)(2,1)} %w_ref.1), custom_call_target="tpu_custom_call" | custom-call | tf_op jit(solution)/shard_map/sparse_attention/pallas_call | solution.py:517
  108.9 1.8 %copy.8 = bf16[48,5120]{1,0:T(8,128)(2,1)} copy(bf16[48,5120]{1,0:T(8,128)(2,1)} %sparse_attention.1) | data formatting | bytes 983040
